TPU v7x, 128 devices: a whole 4x4x4 slice. The times are simulated.
128 devices in a mesh: region: 4 (over z_hi, core), tile: 32 (over x, z_lo, y).
Axes of the slice: x: 4, y: 4, z: 4 (z_hi: 2, z_lo: 2; z = z_hi * 2 + z_lo), core: 2. Of those that a mesh axis runs over, the one named last changes fastest.
Arguments:
- pts_coords: float32 [32768, 2, 256], P(('region', 'tile')), may hold values from 0 to 127
- pts_height: float32 [32768, 256], P(('region', 'tile')), may hold values from -7 to 7
- pts_weight: float32 [32768, 256], P(('region', 'tile')), may hold values from 0.25 to 4
- block_dest: int32 [32768, 1], P(('region', 'tile')), may hold values from 0 to 31; in each aligned block of 256 rows (0 to 255, 256 to 511, ...) at most 16 rows name the same one
- block_count: int32 [32768], P(('region', 'tile')), may hold values from 64 to 256
- ground_mask: int32 [32768, 256], P(('region', 'tile')), may hold values 0 or 1
- fixed_mask: int32 [4096, 512], P('tile', 'region'), may hold values 0 or 1
Outputs:
- terrain: float32 [4096, 512], P('tile', 'region')
- ground_weight: float32 [4096, 512], P('tile', 'region')
Inputs may be any that keep to these rules, and one draw needn't show every extreme that they name: `block_dest`: among the 256 blocks of one device, no tile is named by more than 16 blocks, a bound that some block reaches.
All inputs are finite; a program needn't handle non-finite values. No bound on the sum of `ground_mask` or of `fixed_mask` on one device may be relied on, other than what follows from the above.
Results may differ from a plain program's by a relative error of at most 0.0003.
The roundings to bfloat16 on the way count: a program that leaves them out, or rounds other values in their place, can miss the bound.
Values sent between devices are 32-bit elements; how exact they have to be, the bound alone decides.
A program may use at most 64 MiB of HBM per device.

v0:
```python
import jax
import jax.numpy as jnp
from jax import lax
from jax.sharding import PartitionSpec as P

PB = 16
SWEEPS = 8


stiffness = 1.0
relaxation = 0.5
base_slack = 0.3
slope_slack = 1.0
softness = 0.2


def extended(cells, sides, width):
    for axis, dim in sides:
        count = lax.axis_size(axis)
        ends = count - 1
        head = lax.slice_in_dim(cells, 0, width, axis=dim)
        tail = lax.slice_in_dim(cells, cells.shape[dim] - width, cells.shape[dim], axis=dim)
        cells = jnp.concatenate(
            [
                lax.ppermute(tail, axis, [(i, (i + 1) % count) for i in range(ends)]),
                cells,
                lax.ppermute(head, axis, [((i + 1) % count, i) for i in range(ends)]),
            ],
            axis=dim,
        )
    return cells


def splat_points(coord_x, coord_y, weight, height, side_cells):
    anchor = jnp.arange(side_cells, dtype=jnp.float32)
    tent_x = jnp.maximum(0.0, 1.0 - jnp.abs(coord_x[:, None] - anchor[None, :]))
    tent_y = jnp.maximum(0.0, 1.0 - jnp.abs(coord_y[:, None] - anchor[None, :]))
    lifted = weight * height
    left = jnp.stack([weight[:, None] * tent_x, lifted[:, None] * tent_x]).astype(jnp.bfloat16)
    right = tent_y.astype(jnp.bfloat16)
    return jnp.einsum("kma,mb->kab", left, right, preferred_element_type=jnp.float32)


def splat_blocks(blocks, side_cells):
    return splat_points(
        blocks[:, 0, :].reshape(-1),
        blocks[:, 1, :].reshape(-1),
        blocks[:, 2, :].reshape(-1),
        blocks[:, 3, :].reshape(-1),
        side_cells,
    )


def stencil(padded):
    centre = padded[2:-2, 2:-2]
    nearest = padded[1:-3, 2:-2] + padded[3:-1, 2:-2] + padded[2:-2, 1:-3] + padded[2:-2, 3:-1]
    diagonal = padded[1:-3, 1:-3] + padded[1:-3, 3:-1] + padded[3:-1, 1:-3] + padded[3:-1, 3:-1]
    farther = padded[:-4, 2:-2] + padded[4:, 2:-2] + padded[2:-2, :-4] + padded[2:-2, 4:]
    return 20.0 * centre - 8.0 * nearest + 2.0 * diagonal + farther


def relax_cells(centre, padded, density, heights):
    residue = heights - density * centre - stiffness * stencil(padded)
    return centre + relaxation * residue / (density + 20.0 * stiffness)


def on_device(pts_coords, pts_height, pts_weight, block_dest, block_count, ground_mask, fixed_mask):
    n_tile = lax.axis_size("tile")
    tile_id = lax.axis_index("tile")
    side_cells = fixed_mask.shape[0]
    blocks = pts_coords.shape[0]
    points = pts_coords.shape[2]
    capacity = 2 * blocks // n_tile
    slots = jnp.arange(points, dtype=jnp.int32)
    is_live = (slots[None, :] < block_count[:, None]) & (ground_mask == 1)
    weight = jnp.where(is_live, pts_weight, 0.0)
    payload = jnp.stack([pts_coords[:, 0, :], pts_coords[:, 1, :], weight, pts_height], axis=1)
    target = block_dest[:, 0]
    onehot = (target[:, None] == jnp.arange(n_tile, dtype=jnp.int32)[None, :]).astype(jnp.int32)
    order_in = jnp.sum((jnp.cumsum(onehot, axis=0) - onehot) * onehot, axis=1)
    slot_index = target * capacity + order_in
    outbox = jnp.zeros((n_tile * capacity, 4, points), jnp.float32).at[slot_index].set(payload)
    outbox = outbox.reshape(n_tile, capacity, 4, points)
    inbox = lax.all_to_all(outbox, "tile", split_axis=0, concat_axis=0, tiled=True)
    grouped = inbox.reshape(-1, 32, 4, points)

    def add_group(total, group_blocks):
        return (total + splat_blocks(group_blocks, side_cells), None)

    grids, _ = lax.scan(add_group, jnp.zeros((2, side_cells, side_cells), jnp.float32), grouped)
    density = grids[0]
    heights = grids[1]
    terrain = heights / (density + 1.0)
    for sweep_no in range(SWEEPS):
        padded = extended(terrain, (("region", 1), ("tile", 0)), 2)
        terrain = relax_cells(terrain, padded, density, heights)
    panel_rows = side_cells // PB
    panels = terrain.reshape(panel_rows, PB, panel_rows, PB).sum(axis=(1, 3)) * (1.0 / (PB * PB))
    all_panels = n_tile * panel_rows
    reach_x = all_panels / 4.0
    reach_y = panel_rows / 2.0
    rows_y = jnp.arange(panel_rows, dtype=jnp.float32)
    kernel_y = jnp.exp(-((rows_y[:, None] - rows_y[None, :]) ** 2) / (2.0 * reach_y * reach_y))
    own_rows = (tile_id * panel_rows + jnp.arange(panel_rows, dtype=jnp.int32)).astype(jnp.float32)
    every_row = jnp.arange(all_panels, dtype=jnp.float32)
    kernel_own = jnp.exp(
        -((own_rows[:, None] - every_row[None, :]) ** 2) / (2.0 * reach_x * reach_x)
    )
    denom = jnp.sum(kernel_own, axis=1)[:, None] * jnp.sum(kernel_y, axis=1)[None, :]
    piece = lax.all_gather(panels, "tile", axis=0, tiled=True)
    cols = jnp.arange(piece.shape[0], dtype=jnp.int32).astype(jnp.float32)
    kernel_part = jnp.exp(-((own_rows[:, None] - cols[None, :]) ** 2) / (2.0 * reach_x * reach_x))
    smooth_y = jnp.dot(piece, kernel_y.T, precision=lax.Precision.HIGHEST)
    numer = jnp.dot(kernel_part, smooth_y, precision=lax.Precision.HIGHEST)
    trend = numer / denom
    limit = base_slack + slope_slack * jnp.abs(panels - trend)
    limit = jnp.repeat(jnp.repeat(limit, PB, axis=0), PB, axis=1)
    limit = jnp.where(fixed_mask == 1, base_slack, limit)
    misfit = jnp.abs(heights - density * terrain) / (density + 1.0)
    ground_weight = jax.nn.sigmoid((limit - misfit) / softness)
    return (terrain, ground_weight)


def solution(mesh):
    placed = (
        P(("region", "tile"), None, None),
        P(("region", "tile"), None),
        P(("region", "tile"), None),
        P(("region", "tile"), None),
        P(("region", "tile")),
        P(("region", "tile"), None),
        P("tile", "region"),
    )
    return jax.shard_map(
        on_device,
        mesh=mesh,
        in_specs=placed,
        out_specs=(P("tile", "region"), P("tile", "region")),
        check_vma=False,
    )
```

profile of v0, /device:TPU:0, one launch (start us, length us, event | category | flops | bytes accessed | tf_op | source)
XLA Modules:
  0.0 408.7 jit_solution(4026111247126534424)
XLA Ops:
  8.6 23.8 %scatter_fusion = f32[512,4,256]{2,1,0:T(4,128)} fusion(f32[512,4,256]{2,1,0:T(4,128)} %broadcast_in_dim.19, s32[256]{0:T(256)S(1)} %bitcast.123, f32[256,4,256]{2,1,0:T(4,128)S(1)} %pad_maximum_fusion), kind=kCustom, calls=%fused_computation | custom fusion | bytes 3146752 | tf_op jit(solution)/shard_map/scatter | solution.py:82
  32.4 8.9 %all-to-all-start = ((f32[32,16,4,256]{3,2,1,0:T(4,128)}), f32[32,16,4,256]{3,2,1,0:T(4,128)}, u32[]{:S(2)}, u32[]{:S(2)}) async-start(f32[32,16,4,256]{3,2,1,0:T(4,128)} %bitcast.7), calls=%async_computation | async-start | bytes 4194304 | tf_op jit(solution)/shard_map/all_to_all | solution.py:84
  41.4 28.1 %all-to-all-done = f32[32,16,4,256]{3,2,1,0:T(4,128)} async-done(((f32[32,16,4,256]{3,2,1,0:T(4,128)}), f32[32,16,4,256]{3,2,1,0:T(4,128)}, u32[]{:S(2)}, u32[]{:S(2)}) %all-to-all-start) | async-done | bytes 2097184 | tf_op jit(solution)/shard_map/all_to_all | solution.py:84
  69.5 104.9 %while.11 = (s32[]{:T(128)}, f32[2,128,128]{2,1,0:T(8,128)S(1)}, f32[16,32,4,256]{3,2,1,0:T(4,128)}, s32[]{:T(128)}, s32[]{:T(128)}) while((s32[]{:T(128)}, f32[2,128,128]{2,1,0:T(8,128)S(1)}, f32[16,32,4,256]{3,2,1,0:T(4,128)}, s32[]{:T(128)}, s32[]{:T(128)}) %tuple.61), condition=%wide.region_5.6_spmd.clone, body=%wide.region_4.5_spmd.clone.sunk | while | flops 552673280 | bytes 9404491 | solution.py:90
  73.0 3.1 fusion.190
  79.5 3.1 fusion.190
  86.1 3.1 fusion.190
  92.6 3.1 fusion.190
  177.2 5.5 %collective-permute-done.1 = f32[128,2]{0,1:T(2,128)S(1)} collective-permute-done((f32[128,2]{0,1:T(2,128)S(1)}, f32[128,2]{0,1:T(2,128)S(1)}, u32[]{:S(2)}, u32[]{:S(2)}) %collective-permute-start.1) | collective-permute-done | bytes 1056 | tf_op jit(solution)/shard_map/ppermute | solution.py:27
  182.8 4.5 %collective-permute-start.2 = (f32[2,132]{0,1:T(8,128)S(1)}, f32[2,132]{0,1:T(8,128)S(1)}, u32[]{:S(2)}, u32[]{:S(2)}) collective-permute-start(f32[2,132]{0,1:T(8,128)S(1)} %get-tuple-element.64), channel_id=1, source_target_pairs={{0,1},{1,2},{2,3},{3,4},{4,5},{5,6},{6,7},{7,8},{8,9},{9,10},{10,1... | collective-permute-start | bytes 3176 | tf_op jit(solution)/shard_map/ppermute | solution.py:25
  189.2 4.3 %collective-permute-done.3 = f32[2,132]{0,1:T(8,128)S(1)} collective-permute-done((f32[2,132]{0,1:T(8,128)S(1)}, f32[2,132]{0,1:T(8,128)S(1)}, u32[]{:S(2)}, u32[]{:S(2)}) %collective-permute-start.3) | collective-permute-done | bytes 1088 | tf_op jit(solution)/shard_map/ppermute | solution.py:27
  193.8 4.3 %collective-permute-start.4 = (f32[128,2]{0,1:T(2,128)S(1)}, f32[128,2]{0,1:T(2,128)S(1)}, u32[]{:S(2)}, u32[]{:S(2)}) collective-permute-start(f32[128,2]{0,1:T(2,128)S(1)} %get-tuple-element.94), channel_id=1, source_target_pairs={{0,32},{32,64},{64,96},{1,33},{33,65},{65,97},{2,34},{34,66},{66,9... | collective-permute-start | bytes 3080 | tf_op jit(solution)/shard_map/ppermute | solution.py:25
  206.1 4.3 %collective-permute-done.7 = f32[2,132]{0,1:T(8,128)S(1)} collective-permute-done((f32[2,132]{0,1:T(8,128)S(1)}, f32[2,132]{0,1:T(8,128)S(1)}, u32[]{:S(2)}, u32[]{:S(2)}) %collective-permute-start.7) | collective-permute-done | bytes 1088 | tf_op jit(solution)/shard_map/ppermute | solution.py:27
  210.8 4.3 %collective-permute-start.8 = (f32[128,2]{0,1:T(2,128)S(1)}, f32[128,2]{0,1:T(2,128)S(1)}, u32[]{:S(2)}, u32[]{:S(2)}) collective-permute-start(f32[128,2]{0,1:T(2,128)S(1)} %get-tuple-element.92), channel_id=1, source_target_pairs={{0,32},{32,64},{64,96},{1,33},{33,65},{65,97},{2,34},{34,66},{66,9... | collective-permute-start | bytes 3080 | tf_op jit(solution)/shard_map/ppermute | solution.py:25
  219.2 3.8 collective-permute-start.10
  225.0 4.3 %collective-permute-done.11 = f32[2,132]{0,1:T(8,128)S(1)} collective-permute-done((f32[2,132]{0,1:T(8,128)S(1)}, f32[2,132]{0,1:T(8,128)S(1)}, u32[]{:S(2)}, u32[]{:S(2)}) %collective-permute-start.11) | collective-permute-done | bytes 1088 | tf_op jit(solution)/shard_map/ppermute | solution.py:27
  229.6 4.6 %collective-permute-start.12 = (f32[128,2]{0,1:T(2,128)S(1)}, f32[128,2]{0,1:T(2,128)S(1)}, u32[]{:S(2)}, u32[]{:S(2)}) collective-permute-start(f32[128,2]{0,1:T(2,128)S(1)} %get-tuple-element.90), channel_id=1, source_target_pairs={{0,32},{32,64},{64,96},{1,33},{33,65},{65,97},{2,34},{34,66},{66,9... | collective-permute-start | bytes 3080 | tf_op jit(solution)/shard_map/ppermute | solution.py:25
  238.1 4.0 collective-permute-start.14
  244.0 4.3 %collective-permute-done.15 = f32[2,132]{0,1:T(8,128)S(1)} collective-permute-done((f32[2,132]{0,1:T(8,128)S(1)}, f32[2,132]{0,1:T(8,128)S(1)}, u32[]{:S(2)}, u32[]{:S(2)}) %collective-permute-start.15) | collective-permute-done | bytes 1088 | tf_op jit(solution)/shard_map/ppermute | solution.py:27
  248.6 4.6 %collective-permute-start.16 = (f32[128,2]{0,1:T(2,128)S(1)}, f32[128,2]{0,1:T(2,128)S(1)}, u32[]{:S(2)}, u32[]{:S(2)}) collective-permute-start(f32[128,2]{0,1:T(2,128)S(1)} %get-tuple-element.88), channel_id=1, source_target_pairs={{0,32},{32,64},{64,96},{1,33},{33,65},{65,97},{2,34},{34,66},{66,9... | collective-permute-start | bytes 3080 | tf_op jit(solution)/shard_map/ppermute | solution.py:25
  257.1 4.0 collective-permute-start.18
  263.0 4.3 %collective-permute-done.19 = f32[2,132]{0,1:T(8,128)S(1)} collective-permute-done((f32[2,132]{0,1:T(8,128)S(1)}, f32[2,132]{0,1:T(8,128)S(1)}, u32[]{:S(2)}, u32[]{:S(2)}) %collective-permute-start.19) | collective-permute-done | bytes 1088 | tf_op jit(solution)/shard_map/ppermute | solution.py:27
  267.7 4.6 %collective-permute-start.20 = (f32[128,2]{0,1:T(2,128)S(1)}, f32[128,2]{0,1:T(2,128)S(1)}, u32[]{:S(2)}, u32[]{:S(2)}) collective-permute-start(f32[128,2]{0,1:T(2,128)S(1)} %get-tuple-element.86), channel_id=1, source_target_pairs={{0,32},{32,64},{64,96},{1,33},{33,65},{65,97},{2,34},{34,66},{66,9... | collective-permute-start | bytes 3080 | tf_op jit(solution)/shard_map/ppermute | solution.py:25
  276.1 4.6 %collective-permute-start.22 = (f32[2,132]{0,1:T(8,128)S(1)}, f32[2,132]{0,1:T(8,128)S(1)}, u32[]{:S(2)}, u32[]{:S(2)}) collective-permute-start(f32[2,132]{0,1:T(8,128)S(1)} %get-tuple-element.54), channel_id=1, source_target_pairs={{0,1},{1,2},{2,3},{3,4},{4,5},{5,6},{6,7},{7,8},{8,9},{9,10},{10,1... | collective-permute-start | bytes 3176 | tf_op jit(solution)/shard_map/ppermute | solution.py:25
  282.7 4.3 %collective-permute-done.23 = f32[2,132]{0,1:T(8,128)S(1)} collective-permute-done((f32[2,132]{0,1:T(8,128)S(1)}, f32[2,132]{0,1:T(8,128)S(1)}, u32[]{:S(2)}, u32[]{:S(2)}) %collective-permute-start.23) | collective-permute-done | bytes 1088 | tf_op jit(solution)/shard_map/ppermute | solution.py:27
  287.3 4.6 %collective-permute-start.24 = (f32[128,2]{0,1:T(2,128)S(1)}, f32[128,2]{0,1:T(2,128)S(1)}, u32[]{:S(2)}, u32[]{:S(2)}) collective-permute-start(f32[128,2]{0,1:T(2,128)S(1)} %get-tuple-element.84), channel_id=1, source_target_pairs={{0,32},{32,64},{64,96},{1,33},{33,65},{65,97},{2,34},{34,66},{66,9... | collective-permute-start | bytes 3080 | tf_op jit(solution)/shard_map/ppermute | solution.py:25
  295.8 4.9 %collective-permute-start.26 = (f32[2,132]{0,1:T(8,128)S(1)}, f32[2,132]{0,1:T(8,128)S(1)}, u32[]{:S(2)}, u32[]{:S(2)}) collective-permute-start(f32[2,132]{0,1:T(8,128)S(1)} %get-tuple-element.52), channel_id=1, source_target_pairs={{0,1},{1,2},{2,3},{3,4},{4,5},{5,6},{6,7},{7,8},{8,9},{9,10},{10,1... | collective-permute-start | bytes 3176 | tf_op jit(solution)/shard_map/ppermute | solution.py:25
  302.6 4.3 %collective-permute-done.27 = f32[2,132]{0,1:T(8,128)S(1)} collective-permute-done((f32[2,132]{0,1:T(8,128)S(1)}, f32[2,132]{0,1:T(8,128)S(1)}, u32[]{:S(2)}, u32[]{:S(2)}) %collective-permute-start.27) | collective-permute-done | bytes 1088 | tf_op jit(solution)/shard_map/ppermute | solution.py:27
  307.2 4.6 %collective-permute-start.28 = (f32[128,2]{0,1:T(2,128)S(1)}, f32[128,2]{0,1:T(2,128)S(1)}, u32[]{:S(2)}, u32[]{:S(2)}) collective-permute-start(f32[128,2]{0,1:T(2,128)S(1)} %get-tuple-element.82), channel_id=1, source_target_pairs={{0,32},{32,64},{64,96},{1,33},{33,65},{65,97},{2,34},{34,66},{66,9... | collective-permute-start | bytes 3080 | tf_op jit(solution)/shard_map/ppermute | solution.py:25
  315.7 4.9 %collective-permute-start.30 = (f32[2,132]{0,1:T(8,128)S(1)}, f32[2,132]{0,1:T(8,128)S(1)}, u32[]{:S(2)}, u32[]{:S(2)}) collective-permute-start(f32[2,132]{0,1:T(8,128)S(1)} %get-tuple-element.50), channel_id=1, source_target_pairs={{0,1},{1,2},{2,3},{3,4},{4,5},{5,6},{6,7},{7,8},{8,9},{9,10},{10,1... | collective-permute-start | bytes 3176 | tf_op jit(solution)/shard_map/ppermute | solution.py:25
  322.5 4.3 %collective-permute-done.31 = f32[2,132]{0,1:T(8,128)S(1)} collective-permute-done((f32[2,132]{0,1:T(8,128)S(1)}, f32[2,132]{0,1:T(8,128)S(1)}, u32[]{:S(2)}, u32[]{:S(2)}) %collective-permute-start.31) | collective-permute-done | bytes 1088 | tf_op jit(solution)/shard_map/ppermute | solution.py:27
  328.3 79.0 %all_gather.3 = f32[256,8]{1,0:T(8,128)S(1)} all-gather(f32[8,8]{1,0:T(8,128)S(1)} %broadcast_multiply_fusion), channel_id=1, replica_groups=mesh['region'=4,'tile'=32] {'tile'}, dimensions={0}, use_global_device_ids=true | all-gather | bytes 8448 | tf_op jit(solution)/shard_map/all_gather | solution.py:110
  (193 shorter events, 152.2 us)
Async XLA Ops:
  32.4 37.1 %all-to-all-start = ((f32[32,16,4,256]{3,2,1,0:T(4,128)}), f32[32,16,4,256]{3,2,1,0:T(4,128)}, u32[]{:S(2)}, u32[]{:S(2)}) async-start(f32[32,16,4,256]{3,2,1,0:T(4,128)} %bitcast.7), calls=%async_computation | async-start | bytes 4194304 | tf_op jit(solution)/shard_map/all_to_all | solution.py:84
  175.9 6.8 %collective-permute-start.1 = (f32[128,2]{0,1:T(2,128)S(1)}, f32[128,2]{0,1:T(2,128)S(1)}, u32[]{:S(2)}, u32[]{:S(2)}) collective-permute-start(f32[128,2]{0,1:T(2,128)S(1)} %get-tuple-element.97), channel_id=1, source_target_pairs={{32,0},{64,32},{96,64},{33,1},{65,33},{97,65},{34,2},{66,34},{98,6... | collective-permute-start | bytes 3080 | tf_op jit(solution)/shard_map/ppermute | solution.py:27
  182.8 6.4 %collective-permute-start.2 = (f32[2,132]{0,1:T(8,128)S(1)}, f32[2,132]{0,1:T(8,128)S(1)}, u32[]{:S(2)}, u32[]{:S(2)}) collective-permute-start(f32[2,132]{0,1:T(8,128)S(1)} %get-tuple-element.64), channel_id=1, source_target_pairs={{0,1},{1,2},{2,3},{3,4},{4,5},{5,6},{6,7},{7,8},{8,9},{9,10},{10,1... | collective-permute-start | bytes 3176 | tf_op jit(solution)/shard_map/ppermute | solution.py:25
  187.3 6.2 %collective-permute-start.3 = (f32[2,132]{0,1:T(8,128)S(1)}, f32[2,132]{0,1:T(8,128)S(1)}, u32[]{:S(2)}, u32[]{:S(2)}) collective-permute-start(f32[2,132]{0,1:T(8,128)S(1)} %get-tuple-element.65), channel_id=1, source_target_pairs={{1,0},{2,1},{3,2},{4,3},{5,4},{6,5},{7,6},{8,7},{9,8},{10,9},{11,1... | collective-permute-start | bytes 3176 | tf_op jit(solution)/shard_map/ppermute | solution.py:27
  193.8 5.6 %collective-permute-start.4 = (f32[128,2]{0,1:T(2,128)S(1)}, f32[128,2]{0,1:T(2,128)S(1)}, u32[]{:S(2)}, u32[]{:S(2)}) collective-permute-start(f32[128,2]{0,1:T(2,128)S(1)} %get-tuple-element.94), channel_id=1, source_target_pairs={{0,32},{32,64},{64,96},{1,33},{33,65},{65,97},{2,34},{34,66},{66,9... | collective-permute-start | bytes 3080 | tf_op jit(solution)/shard_map/ppermute | solution.py:25
  198.2 4.0 collective-permute-start.5
  202.3 3.8 collective-permute-start.6
  204.2 6.2 %collective-permute-start.7 = (f32[2,132]{0,1:T(8,128)S(1)}, f32[2,132]{0,1:T(8,128)S(1)}, u32[]{:S(2)}, u32[]{:S(2)}) collective-permute-start(f32[2,132]{0,1:T(8,128)S(1)} %get-tuple-element.63), channel_id=1, source_target_pairs={{1,0},{2,1},{3,2},{4,3},{5,4},{6,5},{7,6},{8,7},{9,8},{10,9},{11,1... | collective-permute-start | bytes 3176 | tf_op jit(solution)/shard_map/ppermute | solution.py:27
  210.8 5.6 %collective-permute-start.8 = (f32[128,2]{0,1:T(2,128)S(1)}, f32[128,2]{0,1:T(2,128)S(1)}, u32[]{:S(2)}, u32[]{:S(2)}) collective-permute-start(f32[128,2]{0,1:T(2,128)S(1)} %get-tuple-element.92), channel_id=1, source_target_pairs={{0,32},{32,64},{64,96},{1,33},{33,65},{65,97},{2,34},{34,66},{66,9... | collective-permute-start | bytes 3080 | tf_op jit(solution)/shard_map/ppermute | solution.py:25
  215.1 4.0 collective-permute-start.9
  219.2 5.8 %collective-permute-start.10 = (f32[2,132]{0,1:T(8,128)S(1)}, f32[2,132]{0,1:T(8,128)S(1)}, u32[]{:S(2)}, u32[]{:S(2)}) collective-permute-start(f32[2,132]{0,1:T(8,128)S(1)} %get-tuple-element.60), channel_id=1, source_target_pairs={{0,1},{1,2},{2,3},{3,4},{4,5},{5,6},{6,7},{7,8},{8,9},{9,10},{10,1... | collective-permute-start | bytes 3176 | tf_op jit(solution)/shard_map/ppermute | solution.py:25
  223.1 6.2 %collective-permute-start.11 = (f32[2,132]{0,1:T(8,128)S(1)}, f32[2,132]{0,1:T(8,128)S(1)}, u32[]{:S(2)}, u32[]{:S(2)}) collective-permute-start(f32[2,132]{0,1:T(8,128)S(1)} %get-tuple-element.61), channel_id=1, source_target_pairs={{1,0},{2,1},{3,2},{4,3},{5,4},{6,5},{7,6},{8,7},{9,8},{10,9},{11,1... | collective-permute-start | bytes 3176 | tf_op jit(solution)/shard_map/ppermute | solution.py:27
  229.6 5.9 %collective-permute-start.12 = (f32[128,2]{0,1:T(2,128)S(1)}, f32[128,2]{0,1:T(2,128)S(1)}, u32[]{:S(2)}, u32[]{:S(2)}) collective-permute-start(f32[128,2]{0,1:T(2,128)S(1)} %get-tuple-element.90), channel_id=1, source_target_pairs={{0,32},{32,64},{64,96},{1,33},{33,65},{65,97},{2,34},{34,66},{66,9... | collective-permute-start | bytes 3080 | tf_op jit(solution)/shard_map/ppermute | solution.py:25
  234.2 3.7 collective-permute-start.13
  238.1 6.0 %collective-permute-start.14 = (f32[2,132]{0,1:T(8,128)S(1)}, f32[2,132]{0,1:T(8,128)S(1)}, u32[]{:S(2)}, u32[]{:S(2)}) collective-permute-start(f32[2,132]{0,1:T(8,128)S(1)} %get-tuple-element.58), channel_id=1, source_target_pairs={{0,1},{1,2},{2,3},{3,4},{4,5},{5,6},{6,7},{7,8},{8,9},{9,10},{10,1... | collective-permute-start | bytes 3176 | tf_op jit(solution)/shard_map/ppermute | solution.py:25
  242.1 6.2 %collective-permute-start.15 = (f32[2,132]{0,1:T(8,128)S(1)}, f32[2,132]{0,1:T(8,128)S(1)}, u32[]{:S(2)}, u32[]{:S(2)}) collective-permute-start(f32[2,132]{0,1:T(8,128)S(1)} %get-tuple-element.59), channel_id=1, source_target_pairs={{1,0},{2,1},{3,2},{4,3},{5,4},{6,5},{7,6},{8,7},{9,8},{10,9},{11,1... | collective-permute-start | bytes 3176 | tf_op jit(solution)/shard_map/ppermute | solution.py:27
  248.6 5.9 %collective-permute-start.16 = (f32[128,2]{0,1:T(2,128)S(1)}, f32[128,2]{0,1:T(2,128)S(1)}, u32[]{:S(2)}, u32[]{:S(2)}) collective-permute-start(f32[128,2]{0,1:T(2,128)S(1)} %get-tuple-element.88), channel_id=1, source_target_pairs={{0,32},{32,64},{64,96},{1,33},{33,65},{65,97},{2,34},{34,66},{66,9... | collective-permute-start | bytes 3080 | tf_op jit(solution)/shard_map/ppermute | solution.py:25
  253.2 3.7 collective-permute-start.17
  257.1 6.0 %collective-permute-start.18 = (f32[2,132]{0,1:T(8,128)S(1)}, f32[2,132]{0,1:T(8,128)S(1)}, u32[]{:S(2)}, u32[]{:S(2)}) collective-permute-start(f32[2,132]{0,1:T(8,128)S(1)} %get-tuple-element.56), channel_id=1, source_target_pairs={{0,1},{1,2},{2,3},{3,4},{4,5},{5,6},{6,7},{7,8},{8,9},{9,10},{10,1... | collective-permute-start | bytes 3176 | tf_op jit(solution)/shard_map/ppermute | solution.py:25
  261.1 6.2 %collective-permute-start.19 = (f32[2,132]{0,1:T(8,128)S(1)}, f32[2,132]{0,1:T(8,128)S(1)}, u32[]{:S(2)}, u32[]{:S(2)}) collective-permute-start(f32[2,132]{0,1:T(8,128)S(1)} %get-tuple-element.57), channel_id=1, source_target_pairs={{1,0},{2,1},{3,2},{4,3},{5,4},{6,5},{7,6},{8,7},{9,8},{10,9},{11,1... | collective-permute-start | bytes 3176 | tf_op jit(solution)/shard_map/ppermute | solution.py:27
  267.7 5.9 %collective-permute-start.20 = (f32[128,2]{0,1:T(2,128)S(1)}, f32[128,2]{0,1:T(2,128)S(1)}, u32[]{:S(2)}, u32[]{:S(2)}) collective-permute-start(f32[128,2]{0,1:T(2,128)S(1)} %get-tuple-element.86), channel_id=1, source_target_pairs={{0,32},{32,64},{64,96},{1,33},{33,65},{65,97},{2,34},{34,66},{66,9... | collective-permute-start | bytes 3080 | tf_op jit(solution)/shard_map/ppermute | solution.py:25
  272.3 3.7 collective-permute-start.21
  276.1 6.6 %collective-permute-start.22 = (f32[2,132]{0,1:T(8,128)S(1)}, f32[2,132]{0,1:T(8,128)S(1)}, u32[]{:S(2)}, u32[]{:S(2)}) collective-permute-start(f32[2,132]{0,1:T(8,128)S(1)} %get-tuple-element.54), channel_id=1, source_target_pairs={{0,1},{1,2},{2,3},{3,4},{4,5},{5,6},{6,7},{7,8},{8,9},{9,10},{10,1... | collective-permute-start | bytes 3176 | tf_op jit(solution)/shard_map/ppermute | solution.py:25
  280.8 6.2 %collective-permute-start.23 = (f32[2,132]{0,1:T(8,128)S(1)}, f32[2,132]{0,1:T(8,128)S(1)}, u32[]{:S(2)}, u32[]{:S(2)}) collective-permute-start(f32[2,132]{0,1:T(8,128)S(1)} %get-tuple-element.55), channel_id=1, source_target_pairs={{1,0},{2,1},{3,2},{4,3},{5,4},{6,5},{7,6},{8,7},{9,8},{10,9},{11,1... | collective-permute-start | bytes 3176 | tf_op jit(solution)/shard_map/ppermute | solution.py:27
  287.3 5.9 %collective-permute-start.24 = (f32[128,2]{0,1:T(2,128)S(1)}, f32[128,2]{0,1:T(2,128)S(1)}, u32[]{:S(2)}, u32[]{:S(2)}) collective-permute-start(f32[128,2]{0,1:T(2,128)S(1)} %get-tuple-element.84), channel_id=1, source_target_pairs={{0,32},{32,64},{64,96},{1,33},{33,65},{65,97},{2,34},{34,66},{66,9... | collective-permute-start | bytes 3080 | tf_op jit(solution)/shard_map/ppermute | solution.py:25
  291.9 3.7 collective-permute-start.25
  295.8 6.9 %collective-permute-start.26 = (f32[2,132]{0,1:T(8,128)S(1)}, f32[2,132]{0,1:T(8,128)S(1)}, u32[]{:S(2)}, u32[]{:S(2)}) collective-permute-start(f32[2,132]{0,1:T(8,128)S(1)} %get-tuple-element.52), channel_id=1, source_target_pairs={{0,1},{1,2},{2,3},{3,4},{4,5},{5,6},{6,7},{7,8},{8,9},{9,10},{10,1... | collective-permute-start | bytes 3176 | tf_op jit(solution)/shard_map/ppermute | solution.py:25
  300.7 6.2 %collective-permute-start.27 = (f32[2,132]{0,1:T(8,128)S(1)}, f32[2,132]{0,1:T(8,128)S(1)}, u32[]{:S(2)}, u32[]{:S(2)}) collective-permute-start(f32[2,132]{0,1:T(8,128)S(1)} %get-tuple-element.53), channel_id=1, source_target_pairs={{1,0},{2,1},{3,2},{4,3},{5,4},{6,5},{7,6},{8,7},{9,8},{10,9},{11,1... | collective-permute-start | bytes 3176 | tf_op jit(solution)/shard_map/ppermute | solution.py:27
  307.2 6.1 %collective-permute-start.28 = (f32[128,2]{0,1:T(2,128)S(1)}, f32[128,2]{0,1:T(2,128)S(1)}, u32[]{:S(2)}, u32[]{:S(2)}) collective-permute-start(f32[128,2]{0,1:T(2,128)S(1)} %get-tuple-element.82), channel_id=1, source_target_pairs={{0,32},{32,64},{64,96},{1,33},{33,65},{65,97},{2,34},{34,66},{66,9... | collective-permute-start | bytes 3080 | tf_op jit(solution)/shard_map/ppermute | solution.py:25
  311.8 3.7 collective-permute-start.29
  315.7 6.9 %collective-permute-start.30 = (f32[2,132]{0,1:T(8,128)S(1)}, f32[2,132]{0,1:T(8,128)S(1)}, u32[]{:S(2)}, u32[]{:S(2)}) collective-permute-start(f32[2,132]{0,1:T(8,128)S(1)} %get-tuple-element.50), channel_id=1, source_target_pairs={{0,1},{1,2},{2,3},{3,4},{4,5},{5,6},{6,7},{7,8},{8,9},{9,10},{10,1... | collective-permute-start | bytes 3176 | tf_op jit(solution)/shard_map/ppermute | solution.py:25
  320.6 6.2 %collective-permute-start.31 = (f32[2,132]{0,1:T(8,128)S(1)}, f32[2,132]{0,1:T(8,128)S(1)}, u32[]{:S(2)}, u32[]{:S(2)}) collective-permute-start(f32[2,132]{0,1:T(8,128)S(1)} %get-tuple-element.51), channel_id=1, source_target_pairs={{1,0},{2,1},{3,2},{4,3},{5,4},{6,5},{7,6},{8,7},{9,8},{10,9},{11,1... | collective-permute-start | bytes 3176 | tf_op jit(solution)/shard_map/ppermute | solution.py:27
  (3 other events, 62.6 us)
where the time goes:
time: 411 us; the launch traced here: 409 us
  starting transfers between devices  95.4 us (23%)
  waiting for transfers between devices  90 us (22%)
  blocking collectives  79 us (19%)
  matrix products  50.2 us (12%)
  local copies, waits for them, and re-layouts  46.1 us (11%)
  other arithmetic  46.1 us (11%)
    all_gather x1, blocking collectives, on_device(): piece = lax.all_gather(panels, 'tile', axis=0, tiled=True)  79 us
    ppermute x16, starting transfers between devices, extended(): lax.ppermute(tail, axis, [(i, (i + 1) % count) for i in range(ends)])  65.8 us
    ppermute x16, waiting for transfers between devices, extended(): lax.ppermute(head, axis, [((i + 1) % count, i) for i in range(ends)])  57.1 us
    dot_general x16, matrix products, splat_points(): jnp.einsum('kma,mb->kab', left, right, preferred_element_type=jnp.float32)  49.8 us
    another operation x18, other arithmetic  38.9 us
    all_to_all x1, waiting for transfers between devices, on_device(): lax.all_to_all(outbox, 'tile', split_axis=0, concat_axis=0, tiled=True)  28.1 us
    scatter x1, local copies, waits for them, and re-layouts, on_device(): jnp.zeros((n_tile * capacity, 4, points), jnp.float32).at[slot_index]  23.8 us
    ppermute x16, starting transfers between devices, extended(): lax.ppermute(head, axis, [((i + 1) % count, i) for i in range(ends)])  20.7 us
  transfers between devices with their start and end apart: 33, of which 25 were waited for; matrix products, arithmetic and copies ran while one was open for 0% of the time, Pallas kernels for 0%

commit v1 on v0

v1 whole, which is shorter than its diff:
```python
import functools

import jax
import jax.numpy as jnp
from jax import lax
from jax.experimental import pallas as pl
from jax.experimental.pallas import tpu as pltpu
from jax.sharding import PartitionSpec as P

MESH = pl.DeviceIdType.MESH
F32 = jnp.float32
BF16 = jnp.bfloat16

PB = 16
SWEEPS = 8
HALO = 2 * SWEEPS
CAP = 16
GROUP = 4

stiffness = 1.0
relaxation = 0.5
base_slack = 0.3
slope_slack = 1.0
softness = 0.2


def iota(shape, dim):
    return lax.broadcasted_iota(jnp.int32, shape, dim)


def tent(coord, anchor):
    return jnp.maximum(0.0, 1.0 - jnp.abs(coord - anchor))


def dot_exact(a, b):
    return jnp.dot(a, b, precision=lax.Precision.HIGHEST, preferred_element_type=F32)


def laplacian(v):
    rows, lanes = v.shape
    near = (
        pltpu.roll(v, 1, 0)
        + pltpu.roll(v, rows - 1, 0)
        + pltpu.roll(v, 1, 1)
        + pltpu.roll(v, lanes - 1, 1)
    )
    return near - 4.0 * v


def kernel(
    n_region,
    n_tile,
    coords_ref,
    height_ref,
    weight_ref,
    dest_ref,
    count_ref,
    ground_ref,
    fixed_ref,
    terrain_ref,
    soft_ref,
    payload,
    outbox,
    inbox,
    left_buf,
    right_buf,
    grids,
    edge,
    from_up,
    from_down,
    from_side,
    field,
    smooth,
    gathered,
    box_send,
    box_recv,
    halo_send,
    halo_recv,
    panel_send,
    panel_recv,
):
    region = lax.axis_index("region")
    tile = lax.axis_index("tile")
    blocks, points = height_ref.shape
    side = fixed_ref.shape[0]
    right = lax.rem(region + 1, n_region)
    left = lax.rem(region + n_region - 1, n_region)
    down = lax.rem(tile + 1, n_tile)
    up = lax.rem(tile + n_tile - 1, n_tile)

    barrier = pltpu.get_barrier_semaphore()

    def greet(shift, carry):
        pl.semaphore_signal(
            barrier, inc=1, device_id=(region, lax.rem(tile + shift, n_tile)), device_id_type=MESH
        )
        return carry

    lax.fori_loop(1, n_tile, greet, 0)
    for other in (left, right):
        for row in (up, tile, down):
            pl.semaphore_signal(barrier, inc=1, device_id=(other, row), device_id_type=MESH)

    eye = iota((blocks, blocks), 0) == iota((blocks, blocks), 1)
    dest_row = dest_ref[...].astype(F32)
    dest_col = jnp.sum(jnp.where(eye, dest_row, 0.0), axis=1, keepdims=True)
    count_col = jnp.sum(jnp.where(eye, count_ref[...].astype(F32), 0.0), axis=1, keepdims=True)
    live = (iota((blocks, points), 1).astype(F32) < count_col) & (ground_ref[...] == 1)
    weight = jnp.where(live, weight_ref[...], 0.0)
    values = (coords_ref[:, 0, :], coords_ref[:, 1, :], weight, weight * height_ref[...])
    for q, value in enumerate(values):
        for part in range(3):
            rounded = value.astype(BF16)
            payload[part * blocks : (part + 1) * blocks, q * points : (q + 1) * points] = rounded
            value = value - rounded.astype(F32)
    earlier = iota((blocks, blocks), 0) < iota((blocks, blocks), 1)
    order = jnp.sum(jnp.where((dest_col == dest_row) & earlier, 1.0, 0.0), axis=0, keepdims=True)
    away = dest_row - tile.astype(F32)
    away = jnp.where(away < 0.0, away + n_tile, away)
    slot_row = away * CAP + order

    pl.semaphore_wait(barrier, n_tile - 1 + 6)

    def box_copy(shift):
        return pltpu.make_async_remote_copy(
            src_ref=outbox.at[shift],
            dst_ref=inbox.at[shift],
            send_sem=box_send.at[shift],
            recv_sem=box_recv.at[shift],
            device_id=(region, lax.rem(tile + shift, n_tile)),
            device_id_type=MESH,
        )

    def pack(group, carry):
        rows = GROUP * CAP
        slots = iota((rows, blocks), 0) + group * rows
        pick = jnp.where(slots.astype(F32) == slot_row, 1.0, 0.0).astype(BF16)
        picked = jnp.dot(jnp.concatenate([pick] * 3, axis=1), payload[...], preferred_element_type=F32)
        first = pl.multiple_of(group * GROUP, GROUP)
        for q in range(4):
            piece = picked[:, q * points : (q + 1) * points].reshape(GROUP, CAP, points)
            outbox[pl.ds(first, GROUP), q * CAP : (q + 1) * CAP, :] = piece
        return carry

    def send_group(group, carry):
        pack(group, carry)

        def send(k, inner):
            @pl.when(group * GROUP + k > 0)
            def _():
                box_copy(group * GROUP + k).start()

            return inner

        return lax.fori_loop(0, GROUP, send, carry)

    lax.fori_loop(0, n_tile // GROUP, send_group, 0)

    inbox[0] = outbox[0]
    grids[...] = jnp.zeros_like(grids)
    anchors = iota((16, points), 0).astype(F32).astype(BF16)
    zero = jnp.zeros((16, points), BF16)

    def splat(shift, carry):
        @pl.when(shift > 0)
        def _():
            box_copy(shift).wait_recv()

        box = inbox[shift]
        x, y, w, u = [box[q * CAP : (q + 1) * CAP, :] for q in range(4)]
        x_low, y_low = jnp.floor(x), jnp.floor(y)
        x_high, y_high = x_low + 1.0, y_low + 1.0
        tx0, tx1 = tent(x, x_low), tent(x, x_high)
        rows = (x_low, x_high, y_low, y_high, w * tx0, w * tx1, u * tx0, u * tx1, tent(y, y_low), tent(y, y_high))
        for j in range(CAP):
            slot, col = (j // 4) % 2, (j % 4) * points
            spread = [jnp.broadcast_to(r[j : j + 1, :], (16, points)).astype(BF16) for r in rows]
            xl, xh, yl, yh, w0, w1, u0, u1, r0, r1 = spread
            for t in range(side // 16):
                at = anchors + BF16(16 * t)
                low, high = at == xl, at == xh
                lanes = slice(col, col + points)
                left_buf[slot, 16 * t : 16 * t + 16, lanes] = jnp.where(low, w0, jnp.where(high, w1, zero))
                left_buf[slot, side + 16 * t : side + 16 * t + 16, lanes] = jnp.where(
                    low, u0, jnp.where(high, u1, zero)
                )
                right_buf[slot, 16 * t : 16 * t + 16, lanes] = jnp.where(
                    at == yl, r0, jnp.where(at == yh, r1, zero)
                )
            if j % 4 == 3:
                grids[...] += lax.dot_general(
                    left_buf[slot], right_buf[slot], (((1,), (1,)), ((), ())), preferred_element_type=F32
                )
        return carry

    lax.fori_loop(0, n_tile, splat, 0)

    density, heights = grids[0:side, :], grids[side : 2 * side, :]
    lane = iota((side, side), 1)
    edge[...] = jnp.where(
        (lane < HALO) | (lane >= side - HALO),
        density,
        jnp.where(lane < 2 * HALO, pltpu.roll(heights, HALO, 1), pltpu.roll(heights, side - HALO, 1)),
    )

    def halo_copy(k, src, dst, device):
        return pltpu.make_async_remote_copy(
            src_ref=src,
            dst_ref=dst,
            send_sem=halo_send.at[k],
            recv_sem=halo_recv.at[k],
            device_id=device,
            device_id_type=MESH,
        )

    last = side - HALO
    copies = [
        halo_copy(0, edge, from_side.at[0], (left, tile)),
        halo_copy(1, edge, from_side.at[1], (right, tile)),
    ]
    for col, other in ((0, region), (1, left), (2, right)):
        for g in range(2):
            k = 2 + 4 * col + 2 * g
            copies.append(
                halo_copy(k, grids.at[pl.ds(g * side, HALO), :], from_down.at[col, g], (other, up))
            )
            copies.append(
                halo_copy(
                    k + 1, grids.at[pl.ds(g * side + last, HALO), :], from_up.at[col, g], (other, down)
                )
            )
    for copy in copies:
        copy.start()

    panels_side = side // PB
    all_panels = n_tile * panels_side
    reach_x = all_panels / 4.0
    reach_y = panels_side / 2.0
    own_row = iota((panels_side, all_panels), 0) + tile * panels_side
    slot = iota((panels_side, all_panels), 1)
    source = tile - slot // panels_side
    source = jnp.where(source < 0, source + n_tile, source)
    gap_x = (own_row - source * panels_side - slot % panels_side).astype(F32)
    kernel_x = jnp.exp(-(gap_x * gap_x) / (2.0 * reach_x * reach_x))
    cell_panel = iota((side, side), 0) // PB
    column = iota((side, side), 1)
    gap_y = (cell_panel - column).astype(F32)
    is_panel = column < panels_side
    area = 1.0 / (PB * PB)
    mean_of = jnp.where(is_panel & (cell_panel == column), area, 0.0)
    smooth_of = jnp.where(is_panel, jnp.exp(-(gap_y * gap_y) / (2.0 * reach_y * reach_y)) * area, 0.0)
    sum_y = jnp.sum(smooth_of, axis=0, keepdims=True) * (1.0 * PB)
    denom = jnp.sum(kernel_x, axis=1, keepdims=True) * jnp.where(iota((1, side), 1) < panels_side, sum_y, 1.0)
    spread_of = jnp.where(iota((side, side), 0) == iota((side, side), 1) // PB, 1.0, 0.0)

    for copy in copies:
        copy.wait()

    rows_all = side + 2 * HALO
    lane = iota((side, side), 1)
    strip = iota((HALO, side), 1)
    to_right, to_left = lane < HALO, lane >= side - HALO
    strip_right, strip_left = strip < HALO, strip >= side - HALO
    for g, (own, of_left, of_right) in enumerate(
        (
            (density, from_side[1], from_side[0]),
            (heights, pltpu.roll(from_side[1], HALO, 1), pltpu.roll(from_side[0], side - HALO, 1)),
        )
    ):
        field[g, HALO : HALO + side, 0:side] = own
        field[g, HALO : HALO + side, side : 2 * side] = jnp.where(
            to_right, of_right, jnp.where(to_left, of_left, 0.0)
        )
        for rows, got in ((slice(0, HALO), from_up), (slice(HALO + side, rows_all), from_down)):
            field[g, rows, 0:side] = got[0, g]
            field[g, rows, side : 2 * side] = jnp.where(
                strip_right, got[1, g], jnp.where(strip_left, got[2, g], 0.0)
            )

    row_at = iota((rows_all, 2 * side), 0) - HALO + tile * side
    lane_at = iota((rows_all, 2 * side), 1)
    col_at = jnp.where(lane_at < side + HALO, lane_at, lane_at - 2 * side) + region * side
    held = (lane_at < side + HALO) | (lane_at >= 2 * side - HALO)
    inside = held & (row_at >= 0) & (row_at < n_tile * side) & (col_at >= 0) & (col_at < n_region * side)
    dens, hts = field[0], field[1]
    field[2] = jnp.where(inside, relaxation / (dens + 20.0 * stiffness), 0.0)
    field[3] = jnp.where(inside, hts / (dens + 1.0), 0.0)

    def sweep(_, carry):
        v = field[3]
        residue = field[1] - field[0] * v - stiffness * laplacian(laplacian(v))
        field[3] = v + field[2] * residue
        return carry

    lax.fori_loop(0, SWEEPS, sweep, 0)
    terrain = field[3, HALO : HALO + side, 0:side]
    terrain_ref[...] = terrain

    sums = jnp.sum(terrain.reshape(panels_side, PB, side), axis=1)
    smooth[...] = dot_exact(sums, smooth_of)

    def panel_copy(shift):
        return pltpu.make_async_remote_copy(
            src_ref=smooth,
            dst_ref=gathered.at[shift],
            send_sem=panel_send.at[shift],
            recv_sem=panel_recv.at[shift],
            device_id=(region, lax.rem(tile + shift, n_tile)),
            device_id_type=MESH,
        )

    def send_panel(shift, carry):
        panel_copy(shift).start()
        return carry

    lax.fori_loop(1, n_tile, send_panel, 0)
    gathered[0] = smooth[...]
    panels = dot_exact(sums, mean_of)
    misfit = jnp.abs(grids[side : 2 * side, :] - grids[0:side, :] * terrain) / (grids[0:side, :] + 1.0)

    def wait_boxes(shift, carry):
        box_copy(shift).wait_send()
        return carry

    lax.fori_loop(1, n_tile, wait_boxes, 0)

    def wait_panel(shift, carry):
        panel_copy(shift).wait()
        return carry

    lax.fori_loop(1, n_tile, wait_panel, 0)
    numer = dot_exact(kernel_x, gathered[...].reshape(all_panels, side))
    limit = base_slack + slope_slack * jnp.abs(panels - numer / denom)
    limit = dot_exact(limit, spread_of)
    limit = jnp.broadcast_to(limit[:, None, :], (panels_side, PB, side)).reshape(side, side)
    limit = jnp.where(fixed_ref[...] == 1, base_slack, limit)
    soft_ref[...] = 1.0 / (1.0 + jnp.exp((misfit - limit) / softness))


def on_device(n_region, n_tile, pts_coords, pts_height, pts_weight, block_dest, block_count, ground_mask, fixed_mask):
    blocks, points = pts_height.shape
    side = fixed_mask.shape[0]
    rows_all = side + 2 * HALO
    panels_side = side // PB
    out = jax.ShapeDtypeStruct((side, side), F32)
    dma = pltpu.SemaphoreType.DMA
    return pl.pallas_call(
        functools.partial(kernel, n_region, n_tile),
        out_shape=(out, out),
        in_specs=[pl.BlockSpec(memory_space=pltpu.VMEM)] * 7,
        out_specs=[pl.BlockSpec(memory_space=pltpu.VMEM)] * 2,
        scratch_shapes=[
            pltpu.VMEM((3 * blocks, 4 * points), BF16),
            pltpu.VMEM((n_tile, 4 * CAP, points), F32),
            pltpu.VMEM((n_tile, 4 * CAP, points), F32),
            pltpu.VMEM((2, 2 * side, 4 * points), BF16),
            pltpu.VMEM((2, side, 4 * points), BF16),
            pltpu.VMEM((2 * side, side), F32),
            pltpu.VMEM((side, side), F32),
            pltpu.VMEM((3, 2, HALO, side), F32),
            pltpu.VMEM((3, 2, HALO, side), F32),
            pltpu.VMEM((2, side, side), F32),
            pltpu.VMEM((4, rows_all, 2 * side), F32),
            pltpu.VMEM((panels_side, side), F32),
            pltpu.VMEM((n_tile, panels_side, side), F32),
            dma((n_tile,)),
            dma((n_tile,)),
            dma((14,)),
            dma((14,)),
            dma((n_tile,)),
            dma((n_tile,)),
        ],
        compiler_params=pltpu.CompilerParams(
            collective_id=0, has_side_effects=True, vmem_limit_bytes=32 << 20
        ),
    )(
        pts_coords,
        pts_height,
        pts_weight,
        block_dest.reshape(1, blocks),
        block_count.reshape(1, blocks),
        ground_mask,
        fixed_mask,
    )


def solution(mesh):
    placed = (
        P(("region", "tile"), None, None),
        P(("region", "tile"), None),
        P(("region", "tile"), None),
        P(("region", "tile"), None),
        P(("region", "tile")),
        P(("region", "tile"), None),
        P("tile", "region"),
    )
    return jax.shard_map(
        functools.partial(on_device, mesh.shape["region"], mesh.shape["tile"]),
        mesh=mesh,
        in_specs=placed,
        out_specs=(P("tile", "region"), P("tile", "region")),
        check_vma=False,
    )
```

time: 411 us -> 84.5 us (0.21)
  the two profiles are of different devices: /device:TPU:0 before, /device:TPU:1 now
where the time goes in v1:
time: 84.5 us; the launch traced here: 84.2 us
  Pallas kernels  76.9 us (91%)
  local copies, waits for them, and re-layouts  6.67 us (8%)
    pallas_call x1, Pallas kernels, on_device(): pl.pallas_call(functools.partial(kernel, n_region, n_tile), out_shape=(ou...  76.9 us
    unnamed x16, local copies, waits for them, and re-layouts  6.67 us

profile of v1, /device:TPU:1, one launch (start us, length us, event | category | flops | bytes accessed | tf_op | source)
XLA Modules:
  0.0 84.2 jit_solution(15252651196867142475)
XLA Ops:
  0.6 0.0 copy-start.6
  0.6 0.0 copy-start.5
  0.7 0.7 copy-done.6
  1.3 0.0 copy-done.5
  1.3 0.0 copy-start
  1.3 1.0 %copy-done = f32[256,2,256]{2,1,0:T(2,128)S(1)} copy-done((f32[256,2,256]{2,1,0:T(2,128)S(1)}, f32[256,2,256]{2,1,0:T(2,128)}, u32[]{:S(2)}) %copy-start) | copy-done | bytes 524312
  2.4 0.0 copy-start.1
  2.4 0.9 %copy-done.1 = f32[256,256]{1,0:T(8,128)S(1)} copy-done((f32[256,256]{1,0:T(8,128)S(1)}, f32[256,256]{1,0:T(8,128)}, u32[]{:S(2)}) %copy-start.1) | copy-done | bytes 262168
  3.3 0.0 copy-start.2
  3.3 0.9 %copy-done.2 = f32[256,256]{1,0:T(8,128)S(1)} copy-done((f32[256,256]{1,0:T(8,128)S(1)}, f32[256,256]{1,0:T(8,128)}, u32[]{:S(2)}) %copy-start.2) | copy-done | bytes 262168
  4.3 0.0 copy-start.3
  4.3 0.9 %copy-done.3 = s32[256,256]{1,0:T(8,128)S(1)} copy-done((s32[256,256]{1,0:T(8,128)S(1)}, s32[256,256]{1,0:T(8,128)}, u32[]{:S(2)}) %copy-start.3) | copy-done | bytes 262168
  5.2 0.0 copy-start.4
  5.2 0.8 copy-done.4
  6.1 76.9 %shard_map.86 = (f32[128,128]{1,0:T(8,128)S(1)}, f32[128,128]{1,0:T(8,128)S(1)}) custom-call(f32[256,2,256]{2,1,0:T(2,128)S(1)} %copy-done, f32[256,256]{1,0:T(8,128)S(1)} %copy-done.1, f32[256,256]{1,0:T(8,128)S(1)} %copy-done.2, s32[1,256]{1,0:T(1,128)S(1)} %bitcast.2, s32[1,256]{1,0:T(1,128)S(1)} %bitcast.3, s32[256,256]{1,0:T(8,128)S(1)} %copy-done.3, ...), custom_call_target="tpu_custom_call" | custom-call | tf_op jit(solution)/shard_map/pallas_call | solution.py:347
  82.9 0.6 copy.11
  83.6 0.6 copy.12
Async XLA Ops:
  0.6 0.7 copy-start.6
  0.6 0.7 copy-start.5
  1.3 1.0 %copy-start = (f32[256,2,256]{2,1,0:T(2,128)S(1)}, f32[256,2,256]{2,1,0:T(2,128)}, u32[]{:S(2)}) copy-start(f32[256,2,256]{2,1,0:T(2,128)} %coords_ref.1) | copy-start | bytes 1572868
  2.4 0.9 %copy-start.1 = (f32[256,256]{1,0:T(8,128)S(1)}, f32[256,256]{1,0:T(8,128)}, u32[]{:S(2)}) copy-start(f32[256,256]{1,0:T(8,128)} %height_ref.1) | copy-start | bytes 786436
  3.3 0.9 %copy-start.2 = (f32[256,256]{1,0:T(8,128)S(1)}, f32[256,256]{1,0:T(8,128)}, u32[]{:S(2)}) copy-start(f32[256,256]{1,0:T(8,128)} %weight_ref.1) | copy-start | bytes 786436
  4.3 0.9 %copy-start.3 = (s32[256,256]{1,0:T(8,128)S(1)}, s32[256,256]{1,0:T(8,128)}, u32[]{:S(2)}) copy-start(s32[256,256]{1,0:T(8,128)} %ground_ref.1) | copy-start | bytes 786436
  5.2 0.8 copy-start.4

commit v2 on v1

--- a/solution.py
+++ b/solution.py
@@ -15,7 +15,8 @@
 SWEEPS = 8
 HALO = 2 * SWEEPS
 CAP = 16
-GROUP = 4
+GROUP = 8
+WINDOW = 8
 
 stiffness = 1.0
 relaxation = 0.5
@@ -30,6 +31,30 @@
 
 def tent(coord, anchor):
     return jnp.maximum(0.0, 1.0 - jnp.abs(coord - anchor))
+
+
+def tile_step(tile, k, n_tile, sign):
+    if n_tile != 32:
+        return lax.rem(tile + sign * k + n_tile, n_tile)
+    group, dx = k // 4, lax.rem(k, 4)
+    dy = lax.rem(dx + group, 4)
+    dz = lax.rem(dx + group + group // 4, 2)
+    x, z, y = tile // 8, lax.rem(tile // 4, 2), lax.rem(tile, 4)
+    x = lax.rem(x + sign * dx + 4, 4)
+    y = lax.rem(y + sign * dy + 4, 4)
+    z = lax.rem(z + dz, 2)
+    return (x * 2 + z) * 4 + y
+
+
+def order_of(dest, tile, n_tile):
+    if n_tile != 32:
+        return (dest - tile + n_tile) & (n_tile - 1)
+    dx = ((dest >> 3) - tile // 8) & 3
+    dz = ((dest >> 2) - tile // 4) & 1
+    dy = (dest - tile) & 3
+    low = (dy - dx) & 3
+    high = (dz ^ dx ^ low) & 1
+    return ((low + 4 * high) << 2) + dx
 
 
 def dot_exact(a, b):
@@ -50,6 +75,15 @@
 def kernel(
     n_region,
     n_tile,
+    coords_hbm,
+    height_hbm,
+    weight_hbm,
+    dest_hbm,
+    count_hbm,
+    ground_hbm,
+    fixed_hbm,
+    terrain_ref,
+    soft_ref,
     coords_ref,
     height_ref,
     weight_ref,
@@ -57,8 +91,6 @@
     count_ref,
     ground_ref,
     fixed_ref,
-    terrain_ref,
-    soft_ref,
     payload,
     outbox,
     inbox,
@@ -78,16 +110,34 @@
     halo_recv,
     panel_send,
     panel_recv,
+    load_sem,
 ):
     region = lax.axis_index("region")
     tile = lax.axis_index("tile")
-    blocks, points = height_ref.shape
-    side = fixed_ref.shape[0]
+    blocks, points = height_hbm.shape
+    side = fixed_hbm.shape[0]
     right = lax.rem(region + 1, n_region)
     left = lax.rem(region + n_region - 1, n_region)
     down = lax.rem(tile + 1, n_tile)
     up = lax.rem(tile + n_tile - 1, n_tile)
 
+    loads = [
+        pltpu.make_async_copy(src, dst, load_sem.at[i])
+        for i, (src, dst) in enumerate(
+            (
+                (dest_hbm, dest_ref),
+                (count_hbm, count_ref),
+                (ground_hbm, ground_ref),
+                (weight_hbm, weight_ref),
+                (height_hbm, height_ref),
+                (coords_hbm, coords_ref),
+                (fixed_hbm, fixed_ref),
+            )
+        )
+    ]
+    for load in loads:
+        load.start()
+
     barrier = pltpu.get_barrier_semaphore()
 
     def greet(shift, carry):
@@ -100,6 +150,9 @@
     for other in (left, right):
         for row in (up, tile, down):
             pl.semaphore_signal(barrier, inc=1, device_id=(other, row), device_id_type=MESH)
+
+    for load in loads:
+        load.wait()
 
     eye = iota((blocks, blocks), 0) == iota((blocks, blocks), 1)
     dest_row = dest_ref[...].astype(F32)
@@ -115,9 +168,7 @@
             value = value - rounded.astype(F32)
     earlier = iota((blocks, blocks), 0) < iota((blocks, blocks), 1)
     order = jnp.sum(jnp.where((dest_col == dest_row) & earlier, 1.0, 0.0), axis=0, keepdims=True)
-    away = dest_row - tile.astype(F32)
-    away = jnp.where(away < 0.0, away + n_tile, away)
-    slot_row = away * CAP + order
+    slot_row = order_of(dest_ref[...], tile, n_tile).astype(F32) * CAP + order
 
     pl.semaphore_wait(barrier, n_tile - 1 + 6)
 
@@ -127,34 +178,39 @@
             dst_ref=inbox.at[shift],
             send_sem=box_send.at[shift],
             recv_sem=box_recv.at[shift],
-            device_id=(region, lax.rem(tile + shift, n_tile)),
+            device_id=(region, tile_step(tile, shift, n_tile, 1)),
             device_id_type=MESH,
         )
 
     def pack(group, carry):
-        rows = GROUP * CAP
+        rows = group_size * CAP
         slots = iota((rows, blocks), 0) + group * rows
         pick = jnp.where(slots.astype(F32) == slot_row, 1.0, 0.0).astype(BF16)
         picked = jnp.dot(jnp.concatenate([pick] * 3, axis=1), payload[...], preferred_element_type=F32)
-        first = pl.multiple_of(group * GROUP, GROUP)
+        first = pl.multiple_of(group * group_size, group_size)
         for q in range(4):
-            piece = picked[:, q * points : (q + 1) * points].reshape(GROUP, CAP, points)
-            outbox[pl.ds(first, GROUP), q * CAP : (q + 1) * CAP, :] = piece
-        return carry
+            piece = picked[:, q * points : (q + 1) * points].reshape(group_size, CAP, points)
+            outbox[pl.ds(first, group_size), q * CAP : (q + 1) * CAP, :] = piece
+        return carry
+
+    group_size = min(GROUP, n_tile)
+    window = min(WINDOW, n_tile - 1)
 
     def send_group(group, carry):
         pack(group, carry)
 
         def send(k, inner):
-            @pl.when(group * GROUP + k > 0)
+            shift = group * group_size + k
+
+            @pl.when((shift > 0) & (shift <= window))
             def _():
-                box_copy(group * GROUP + k).start()
+                box_copy(shift).start()
 
             return inner
 
-        return lax.fori_loop(0, GROUP, send, carry)
-
-    lax.fori_loop(0, n_tile // GROUP, send_group, 0)
+        return lax.fori_loop(0, group_size, send, carry)
+
+    lax.fori_loop(0, n_tile // group_size, send_group, 0)
 
     inbox[0] = outbox[0]
     grids[...] = jnp.zeros_like(grids)
@@ -164,7 +220,12 @@
     def splat(shift, carry):
         @pl.when(shift > 0)
         def _():
+            box_copy(shift).wait_send()
             box_copy(shift).wait_recv()
+
+        @pl.when((shift > 0) & (shift + window < n_tile))
+        def _():
+            box_copy(shift + window).start()
 
         box = inbox[shift]
         x, y, w, u = [box[q * CAP : (q + 1) * CAP, :] for q in range(4)]
@@ -318,12 +379,6 @@
     panels = dot_exact(sums, mean_of)
     misfit = jnp.abs(grids[side : 2 * side, :] - grids[0:side, :] * terrain) / (grids[0:side, :] + 1.0)
 
-    def wait_boxes(shift, carry):
-        box_copy(shift).wait_send()
-        return carry
-
-    lax.fori_loop(1, n_tile, wait_boxes, 0)
-
     def wait_panel(shift, carry):
         panel_copy(shift).wait()
         return carry
@@ -347,9 +402,16 @@
     return pl.pallas_call(
         functools.partial(kernel, n_region, n_tile),
         out_shape=(out, out),
-        in_specs=[pl.BlockSpec(memory_space=pltpu.VMEM)] * 7,
+        in_specs=[pl.BlockSpec(memory_space=pltpu.HBM)] * 7,
         out_specs=[pl.BlockSpec(memory_space=pltpu.VMEM)] * 2,
         scratch_shapes=[
+            pltpu.VMEM(pts_coords.shape, F32),
+            pltpu.VMEM((blocks, points), F32),
+            pltpu.VMEM((blocks, points), F32),
+            pltpu.VMEM((1, blocks), jnp.int32),
+            pltpu.VMEM((1, blocks), jnp.int32),
+            pltpu.VMEM((blocks, points), jnp.int32),
+            pltpu.VMEM((side, side), jnp.int32),
             pltpu.VMEM((3 * blocks, 4 * points), BF16),
             pltpu.VMEM((n_tile, 4 * CAP, points), F32),
             pltpu.VMEM((n_tile, 4 * CAP, points), F32),
@@ -369,6 +431,7 @@
             dma((14,)),
             dma((n_tile,)),
             dma((n_tile,)),
+            dma((7,)),
         ],
         compiler_params=pltpu.CompilerParams(
             collective_id=0, has_side_effects=True, vmem_limit_bytes=32 << 20

time: 84.5 us -> 70.5 us (0.83)
  Pallas kernels: 76.9 us -> 62.9 us
    pallas_call x1, Pallas kernels: 76.9 us -> 62.9 us  [on_device(): pl.pallas_call(functools.partial(kernel, n_region, n_tile), out_shape=(ou...]
where the time goes in v2:
time: 70.5 us; the launch traced here: 70.2 us
  Pallas kernels  62.9 us (89%)
  local copies, waits for them, and re-layouts  6.67 us (9%)
    pallas_call x1, Pallas kernels, on_device(): pl.pallas_call(functools.partial(kernel, n_region, n_tile), out_shape=(ou...  62.9 us
    unnamed x16, local copies, waits for them, and re-layouts  6.67 us

profile of v2, /device:TPU:1, one launch (start us, length us, event | category | flops | bytes accessed | tf_op | source)
XLA Modules:
  0.0 70.2 jit_solution(5954107561176780327)
XLA Ops:
  0.6 0.0 copy-start.6
  0.6 0.0 copy-start.5
  0.7 0.7 copy-done.6
  1.3 0.0 copy-done.5
  1.3 0.0 copy-start
  1.3 1.0 %copy-done = f32[256,2,256]{2,1,0:T(2,128)S(1)} copy-done((f32[256,2,256]{2,1,0:T(2,128)S(1)}, f32[256,2,256]{2,1,0:T(2,128)}, u32[]{:S(2)}) %copy-start) | copy-done | bytes 524312
  2.4 0.0 copy-start.1
  2.4 0.9 %copy-done.1 = f32[256,256]{1,0:T(8,128)S(1)} copy-done((f32[256,256]{1,0:T(8,128)S(1)}, f32[256,256]{1,0:T(8,128)}, u32[]{:S(2)}) %copy-start.1) | copy-done | bytes 262168
  3.3 0.0 copy-start.2
  3.3 0.9 %copy-done.2 = f32[256,256]{1,0:T(8,128)S(1)} copy-done((f32[256,256]{1,0:T(8,128)S(1)}, f32[256,256]{1,0:T(8,128)}, u32[]{:S(2)}) %copy-start.2) | copy-done | bytes 262168
  4.3 0.0 copy-start.3
  4.3 0.9 %copy-done.3 = s32[256,256]{1,0:T(8,128)S(1)} copy-done((s32[256,256]{1,0:T(8,128)S(1)}, s32[256,256]{1,0:T(8,128)}, u32[]{:S(2)}) %copy-start.3) | copy-done | bytes 262168
  5.2 0.0 copy-start.4
  5.2 0.8 %copy-done.4 = s32[128,128]{1,0:T(8,128)S(1)} copy-done((s32[128,128]{1,0:T(8,128)S(1)}, s32[128,128]{1,0:T(8,128)}, u32[]{:S(2)}) %copy-start.4) | copy-done | bytes 65560
  6.1 62.9 %shard_map.86 = (f32[128,128]{1,0:T(8,128)S(1)}, f32[128,128]{1,0:T(8,128)S(1)}) custom-call(f32[256,2,256]{2,1,0:T(2,128)S(1)} %copy-done, f32[256,256]{1,0:T(8,128)S(1)} %copy-done.1, f32[256,256]{1,0:T(8,128)S(1)} %copy-done.2, s32[1,256]{1,0:T(1,128)S(1)} %bitcast.2, s32[1,256]{1,0:T(1,128)S(1)} %bitcast.3, s32[256,256]{1,0:T(8,128)S(1)} %copy-done.3, ...), custom_call_target="tpu_custom_call" | custom-call | tf_op jit(solution)/shard_map/pallas_call | solution.py:402
  69.0 0.6 copy.11
  69.6 0.6 copy.12
Async XLA Ops:
  0.6 0.7 copy-start.6
  0.6 0.7 copy-start.5
  1.3 1.0 %copy-start = (f32[256,2,256]{2,1,0:T(2,128)S(1)}, f32[256,2,256]{2,1,0:T(2,128)}, u32[]{:S(2)}) copy-start(f32[256,2,256]{2,1,0:T(2,128)} %coords_hbm.1) | copy-start | bytes 1572868
  2.4 0.9 %copy-start.1 = (f32[256,256]{1,0:T(8,128)S(1)}, f32[256,256]{1,0:T(8,128)}, u32[]{:S(2)}) copy-start(f32[256,256]{1,0:T(8,128)} %height_hbm.1) | copy-start | bytes 786436
  3.3 0.9 %copy-start.2 = (f32[256,256]{1,0:T(8,128)S(1)}, f32[256,256]{1,0:T(8,128)}, u32[]{:S(2)}) copy-start(f32[256,256]{1,0:T(8,128)} %weight_hbm.1) | copy-start | bytes 786436
  4.3 0.9 %copy-start.3 = (s32[256,256]{1,0:T(8,128)S(1)}, s32[256,256]{1,0:T(8,128)}, u32[]{:S(2)}) copy-start(s32[256,256]{1,0:T(8,128)} %ground_hbm.1) | copy-start | bytes 786436
  5.2 0.8 %copy-start.4 = (s32[128,128]{1,0:T(8,128)S(1)}, s32[128,128]{1,0:T(8,128)}, u32[]{:S(2)}) copy-start(s32[128,128]{1,0:T(8,128)} %fixed_hbm.1) | copy-start | bytes 196612

commit v3 on v2

--- a/solution.py
+++ b/solution.py
@@ -15,8 +15,9 @@
 SWEEPS = 8
 HALO = 2 * SWEEPS
 CAP = 16
-GROUP = 8
-WINDOW = 8
+WINDOW = 14
+PAD = 8
+ROWS = 32
 
 stiffness = 1.0
 relaxation = 0.5
@@ -33,16 +34,37 @@
     return jnp.maximum(0.0, 1.0 - jnp.abs(coord - anchor))
 
 
-def tile_step(tile, k, n_tile, sign):
+def partner_order(n_tile):
     if n_tile != 32:
-        return lax.rem(tile + sign * k + n_tile, n_tile)
-    group, dx = k // 4, lax.rem(k, 4)
-    dy = lax.rem(dx + group, 4)
-    dz = lax.rem(dx + group + group // 4, 2)
+        return list(range(n_tile))
+    load = [0] * 5
+    left = set(range(1, 32))
+    order = [0]
+    while left:
+
+        def after(step):
+            dx, dz, dy = step // 8, step // 4 % 2, step % 4
+            added = (dx in (1, 2), dx in (2, 3), dy in (1, 2), dy in (2, 3), dz)
+            return [have + more for have, more in zip(load, added)]
+
+        step = min(left, key=lambda c: (max(after(c)), sum(after(c)), sum(v * v for v in after(c)), c))
+        load = after(step)
+        left.remove(step)
+        order.append(step)
+    return order
+
+
+def tile_step(tile, k, n_tile):
+    order = partner_order(n_tile)
+    step = order[0]
+    for place in range(1, n_tile):
+        step = jnp.where(k == place, order[place], step)
+    if n_tile != 32:
+        return lax.rem(tile + step, n_tile)
     x, z, y = tile // 8, lax.rem(tile // 4, 2), lax.rem(tile, 4)
-    x = lax.rem(x + sign * dx + 4, 4)
-    y = lax.rem(y + sign * dy + 4, 4)
-    z = lax.rem(z + dz, 2)
+    x = lax.rem(x + step // 8, 4)
+    z = lax.rem(z + step // 4, 2)
+    y = lax.rem(y + step, 4)
     return (x * 2 + z) * 4 + y
 
 
@@ -52,24 +74,31 @@
     dx = ((dest >> 3) - tile // 8) & 3
     dz = ((dest >> 2) - tile // 4) & 1
     dy = (dest - tile) & 3
-    low = (dy - dx) & 3
-    high = (dz ^ dx ^ low) & 1
-    return ((low + 4 * high) << 2) + dx
+    step = dx * 8 + dz * 4 + dy
+    place = jnp.zeros_like(step)
+    for at, candidate in enumerate(partner_order(n_tile)):
+        place = jnp.where(step == candidate, at, place)
+    return place
 
 
 def dot_exact(a, b):
     return jnp.dot(a, b, precision=lax.Precision.HIGHEST, preferred_element_type=F32)
 
 
-def laplacian(v):
-    rows, lanes = v.shape
-    near = (
-        pltpu.roll(v, 1, 0)
-        + pltpu.roll(v, rows - 1, 0)
-        + pltpu.roll(v, 1, 1)
-        + pltpu.roll(v, lanes - 1, 1)
-    )
-    return near - 4.0 * v
+def laplacian(cells, first):
+    side = cells.shape[2]
+    lane = iota((ROWS, side), 1)
+    centre = [cells[k, PAD + first : PAD + first + ROWS, :] for k in range(2)]
+    after = [pltpu.roll(c, 1, 1) for c in centre]
+    before = [pltpu.roll(c, side - 1, 1) for c in centre]
+    out = []
+    for k in range(2):
+        west = jnp.where(lane == 0, after[1 - k], after[k])
+        east = jnp.where(lane == side - 1, before[1 - k], before[k])
+        north = cells[k, PAD + first - 1 : PAD + first - 1 + ROWS, :]
+        south = cells[k, PAD + first + 1 : PAD + first + 1 + ROWS, :]
+        out.append((west + east) + (north + south) - 4.0 * centre[k])
+    return out
 
 
 def kernel(
@@ -98,10 +127,14 @@
     right_buf,
     grids,
     edge,
+    edge_turned,
     from_up,
     from_down,
     from_side,
+    corner,
     field,
+    cells,
+    curved,
     smooth,
     gathered,
     box_send,
@@ -170,47 +203,32 @@
     order = jnp.sum(jnp.where((dest_col == dest_row) & earlier, 1.0, 0.0), axis=0, keepdims=True)
     slot_row = order_of(dest_ref[...], tile, n_tile).astype(F32) * CAP + order
 
-    pl.semaphore_wait(barrier, n_tile - 1 + 6)
-
     def box_copy(shift):
         return pltpu.make_async_remote_copy(
             src_ref=outbox.at[shift],
             dst_ref=inbox.at[shift],
             send_sem=box_send.at[shift],
             recv_sem=box_recv.at[shift],
-            device_id=(region, tile_step(tile, shift, n_tile, 1)),
+            device_id=(region, tile_step(tile, shift, n_tile)),
             device_id_type=MESH,
         )
 
-    def pack(group, carry):
-        rows = group_size * CAP
-        slots = iota((rows, blocks), 0) + group * rows
+    window = min(WINDOW, n_tile - 1)
+    half = n_tile // 2
+    for first in (0, half):
+        slots = iota((half * CAP, blocks), 0) + first * CAP
         pick = jnp.where(slots.astype(F32) == slot_row, 1.0, 0.0).astype(BF16)
-        picked = jnp.dot(jnp.concatenate([pick] * 3, axis=1), payload[...], preferred_element_type=F32)
-        first = pl.multiple_of(group * group_size, group_size)
+        pick = jnp.concatenate([pick] * 3, axis=1)
         for q in range(4):
-            piece = picked[:, q * points : (q + 1) * points].reshape(group_size, CAP, points)
-            outbox[pl.ds(first, group_size), q * CAP : (q + 1) * CAP, :] = piece
-        return carry
-
-    group_size = min(GROUP, n_tile)
-    window = min(WINDOW, n_tile - 1)
-
-    def send_group(group, carry):
-        pack(group, carry)
-
-        def send(k, inner):
-            shift = group * group_size + k
-
-            @pl.when((shift > 0) & (shift <= window))
-            def _():
-                box_copy(shift).start()
-
-            return inner
-
-        return lax.fori_loop(0, group_size, send, carry)
-
-    lax.fori_loop(0, n_tile // group_size, send_group, 0)
+            picked = jnp.dot(pick, payload[:, q * points : (q + 1) * points], preferred_element_type=F32)
+            outbox[first : first + half, q * CAP : (q + 1) * CAP, :] = picked.reshape(half, CAP, points)
+    pl.semaphore_wait(barrier, n_tile - 1 + 6)
+
+    def send(shift, carry):
+        box_copy(shift).start()
+        return carry
+
+    lax.fori_loop(1, window + 1, send, 0)
 
     inbox[0] = outbox[0]
     grids[...] = jnp.zeros_like(grids)
@@ -251,18 +269,21 @@
             if j % 4 == 3:
                 grids[...] += lax.dot_general(
                     left_buf[slot], right_buf[slot], (((1,), (1,)), ((), ())), preferred_element_type=F32
-                )
+                ).reshape(2, side, side)
         return carry
 
     lax.fori_loop(0, n_tile, splat, 0)
 
-    density, heights = grids[0:side, :], grids[side : 2 * side, :]
+    density, heights = grids[0], grids[1]
+    last = side - HALO
     lane = iota((side, side), 1)
-    edge[...] = jnp.where(
-        (lane < HALO) | (lane >= side - HALO),
+    both = jnp.where(
+        (lane < HALO) | (lane >= last),
         density,
-        jnp.where(lane < 2 * HALO, pltpu.roll(heights, HALO, 1), pltpu.roll(heights, side - HALO, 1)),
+        jnp.where(lane < 2 * HALO, pltpu.roll(heights, HALO, 1), pltpu.roll(heights, last, 1)),
     )
+    edge[...] = both
+    edge_turned[...] = both.T
 
     def halo_copy(k, src, dst, device):
         return pltpu.make_async_remote_copy(
@@ -274,22 +295,17 @@
             device_id_type=MESH,
         )
 
-    last = side - HALO
+    head, tail = pl.ds(0, HALO), pl.ds(last, HALO)
     copies = [
-        halo_copy(0, edge, from_side.at[0], (left, tile)),
-        halo_copy(1, edge, from_side.at[1], (right, tile)),
+        halo_copy(0, edge.at[head, :], corner.at[0], (left, up)),
+        halo_copy(1, edge.at[head, :], corner.at[1], (right, up)),
+        halo_copy(2, edge.at[tail, :], corner.at[2], (left, down)),
+        halo_copy(3, edge.at[tail, :], corner.at[3], (right, down)),
+        halo_copy(4, edge_turned.at[pl.ds(0, 2 * HALO), :], from_side.at[0], (left, tile)),
+        halo_copy(5, edge_turned.at[pl.ds(side - 2 * HALO, 2 * HALO), :], from_side.at[1], (right, tile)),
+        halo_copy(6, grids.at[:, head, :], from_down, (region, up)),
+        halo_copy(7, grids.at[:, tail, :], from_up, (region, down)),
     ]
-    for col, other in ((0, region), (1, left), (2, right)):
-        for g in range(2):
-            k = 2 + 4 * col + 2 * g
-            copies.append(
-                halo_copy(k, grids.at[pl.ds(g * side, HALO), :], from_down.at[col, g], (other, up))
-            )
-            copies.append(
-                halo_copy(
-                    k + 1, grids.at[pl.ds(g * side + last, HALO), :], from_up.at[col, g], (other, down)
-                )
-            )
     for copy in copies:
         copy.start()
 
@@ -314,47 +330,55 @@
     denom = jnp.sum(kernel_x, axis=1, keepdims=True) * jnp.where(iota((1, side), 1) < panels_side, sum_y, 1.0)
     spread_of = jnp.where(iota((side, side), 0) == iota((side, side), 1) // PB, 1.0, 0.0)
 
+    rows_all = side + 2 * HALO
+    cells[...] = jnp.zeros_like(cells)
+    curved[...] = jnp.zeros_like(curved)
+    row_at = iota((rows_all, side), 0) - HALO + tile * side
+    lane_at = iota((rows_all, side), 1)
+    row_inside = (row_at >= 0) & (row_at < n_tile * side)
+    side_inside = ((lane_at < HALO) & (region < n_region - 1)) | ((lane_at >= last) & (region > 0))
+    insides = (row_inside, row_inside & side_inside)
+    strip = iota((HALO, side), 1)
+    middle = jnp.zeros((side - 2 * HALO, side), F32)
+
     for copy in copies:
         copy.wait()
 
-    rows_all = side + 2 * HALO
-    lane = iota((side, side), 1)
-    strip = iota((HALO, side), 1)
-    to_right, to_left = lane < HALO, lane >= side - HALO
-    strip_right, strip_left = strip < HALO, strip >= side - HALO
-    for g, (own, of_left, of_right) in enumerate(
-        (
-            (density, from_side[1], from_side[0]),
-            (heights, pltpu.roll(from_side[1], HALO, 1), pltpu.roll(from_side[0], side - HALO, 1)),
-        )
-    ):
-        field[g, HALO : HALO + side, 0:side] = own
-        field[g, HALO : HALO + side, side : 2 * side] = jnp.where(
-            to_right, of_right, jnp.where(to_left, of_left, 0.0)
-        )
-        for rows, got in ((slice(0, HALO), from_up), (slice(HALO + side, rows_all), from_down)):
-            field[g, rows, 0:side] = got[0, g]
-            field[g, rows, side : 2 * side] = jnp.where(
-                strip_right, got[1, g], jnp.where(strip_left, got[2, g], 0.0)
+    for g, own in enumerate((density, heights)):
+        field[g, 0, HALO : HALO + side, :] = own
+        field[g, 0, 0:HALO, :] = from_up[g]
+        field[g, 0, HALO + side : rows_all, :] = from_down[g]
+        of_right = from_side[0, g * HALO : (g + 1) * HALO, :]
+        of_left = from_side[1, (1 - g) * HALO : (2 - g) * HALO, :]
+        field[g, 1, HALO : HALO + side, :] = jnp.concatenate([of_right, middle, of_left], axis=0).T
+        for rows, pair in ((slice(0, HALO), (2, 3)), (slice(HALO + side, rows_all), (0, 1))):
+            of_right, of_left = corner[pair[0]], corner[pair[1]]
+            if g == 1:
+                of_right, of_left = pltpu.roll(of_right, last, 1), pltpu.roll(of_left, HALO, 1)
+            field[g, 1, rows, :] = jnp.where(
+                strip < HALO, of_right, jnp.where(strip >= last, of_left, 0.0)
             )
-
-    row_at = iota((rows_all, 2 * side), 0) - HALO + tile * side
-    lane_at = iota((rows_all, 2 * side), 1)
-    col_at = jnp.where(lane_at < side + HALO, lane_at, lane_at - 2 * side) + region * side
-    held = (lane_at < side + HALO) | (lane_at >= 2 * side - HALO)
-    inside = held & (row_at >= 0) & (row_at < n_tile * side) & (col_at >= 0) & (col_at < n_region * side)
-    dens, hts = field[0], field[1]
-    field[2] = jnp.where(inside, relaxation / (dens + 20.0 * stiffness), 0.0)
-    field[3] = jnp.where(inside, hts / (dens + 1.0), 0.0)
+    for k, inside in enumerate(insides):
+        dens, hts = field[0, k], field[1, k]
+        field[2, k] = jnp.where(inside, relaxation / (dens + 20.0 * stiffness), 0.0)
+        cells[k, PAD : PAD + rows_all, :] = jnp.where(inside, hts / (dens + 1.0), 0.0)
 
     def sweep(_, carry):
-        v = field[3]
-        residue = field[1] - field[0] * v - stiffness * laplacian(laplacian(v))
-        field[3] = v + field[2] * residue
+        for first in range(0, rows_all, ROWS):
+            bent = laplacian(cells, first)
+            for k in range(2):
+                curved[k, PAD + first : PAD + first + ROWS, :] = bent[k]
+        for first in range(0, rows_all, ROWS):
+            bent = laplacian(curved, first)
+            rows = slice(first, first + ROWS)
+            for k in range(2):
+                v = cells[k, PAD + first : PAD + first + ROWS, :]
+                residue = field[1, k, rows, :] - field[0, k, rows, :] * v - stiffness * bent[k]
+                cells[k, PAD + first : PAD + first + ROWS, :] = v + field[2, k, rows, :] * residue
         return carry
 
     lax.fori_loop(0, SWEEPS, sweep, 0)
-    terrain = field[3, HALO : HALO + side, 0:side]
+    terrain = cells[0, PAD + HALO : PAD + HALO + side, :]
     terrain_ref[...] = terrain
 
     sums = jnp.sum(terrain.reshape(panels_side, PB, side), axis=1)
@@ -377,7 +401,7 @@
     lax.fori_loop(1, n_tile, send_panel, 0)
     gathered[0] = smooth[...]
     panels = dot_exact(sums, mean_of)
-    misfit = jnp.abs(grids[side : 2 * side, :] - grids[0:side, :] * terrain) / (grids[0:side, :] + 1.0)
+    misfit = jnp.abs(grids[1] - grids[0] * terrain) / (grids[0] + 1.0)
 
     def wait_panel(shift, carry):
         panel_copy(shift).wait()
@@ -417,24 +441,28 @@
             pltpu.VMEM((n_tile, 4 * CAP, points), F32),
             pltpu.VMEM((2, 2 * side, 4 * points), BF16),
             pltpu.VMEM((2, side, 4 * points), BF16),
-            pltpu.VMEM((2 * side, side), F32),
+            pltpu.VMEM((2, side, side), F32),
             pltpu.VMEM((side, side), F32),
-            pltpu.VMEM((3, 2, HALO, side), F32),
-            pltpu.VMEM((3, 2, HALO, side), F32),
-            pltpu.VMEM((2, side, side), F32),
-            pltpu.VMEM((4, rows_all, 2 * side), F32),
+            pltpu.VMEM((side, side), F32),
+            pltpu.VMEM((2, HALO, side), F32),
+            pltpu.VMEM((2, HALO, side), F32),
+            pltpu.VMEM((2, 2 * HALO, side), F32),
+            pltpu.VMEM((4, HALO, side), F32),
+            pltpu.VMEM((3, 2, rows_all, side), F32),
+            pltpu.VMEM((2, rows_all + 2 * PAD, side), F32),
+            pltpu.VMEM((2, rows_all + 2 * PAD, side), F32),
             pltpu.VMEM((panels_side, side), F32),
             pltpu.VMEM((n_tile, panels_side, side), F32),
             dma((n_tile,)),
             dma((n_tile,)),
-            dma((14,)),
-            dma((14,)),
+            dma((8,)),
+            dma((8,)),
             dma((n_tile,)),
             dma((n_tile,)),
             dma((7,)),
         ],
         compiler_params=pltpu.CompilerParams(
-            collective_id=0, has_side_effects=True, vmem_limit_bytes=32 << 20
+            collective_id=0, has_side_effects=True, vmem_limit_bytes=60 << 20
         ),
     )(
         pts_coords,

time: 70.5 us -> 59.2 us (0.84)
  Pallas kernels: 62.9 us -> 56.2 us
  local copies, waits for them, and re-layouts: 6.67 us -> 2.14 us
    pallas_call x1, Pallas kernels: 62.9 us -> 56.2 us  [on_device(): pl.pallas_call(functools.partial(kernel, n_region, n_tile), out_shape=(ou...]
    unnamed x16 -> x4, local copies, waits for them, and re-layouts: 6.67 us -> 2.14 us
where the time goes in v3:
time: 59.2 us; the launch traced here: 59 us
  Pallas kernels  56.2 us (95%)
  local copies, waits for them, and re-layouts  2.14 us (4%)
  between operations  0.65 us (1%)
    pallas_call x1, Pallas kernels, on_device(): pl.pallas_call(functools.partial(kernel, n_region, n_tile), out_shape=(ou...  56.2 us
    unnamed x4, local copies, waits for them, and re-layouts  2.14 us

profile of v3, /device:TPU:1, one launch (start us, length us, event | category | flops | bytes accessed | tf_op | source)
XLA Modules:
  0.0 59.0 jit_solution(8538812812377841856)
XLA Ops:
  0.6 56.2 %shard_map.86 = (f32[128,128]{1,0:T(8,128)}, f32[128,128]{1,0:T(8,128)}) custom-call(f32[256,2,256]{2,1,0:T(2,128)} %coords_hbm.1, f32[256,256]{1,0:T(8,128)} %height_hbm.1, f32[256,256]{1,0:T(8,128)} %weight_hbm.1, s32[1,256]{1,0:T(1,128)} %bitcast.2, s32[1,256]{1,0:T(1,128)} %bitcast.3, s32[256,256]{1,0:T(8,128)} %ground_hbm.1, s32[128,128]{1,0:T(8,128)} %fixed_hbm.1), custom_call_target="tpu_custom_call" | custom-call | tf_op jit(solution)/shard_map/pallas_call | solution.py:426
  56.8 0.0 copy-start
  56.8 1.5 %copy.11 = f32[128,128]{1,0:T(8,128)} copy(f32[128,128]{1,0:T(8,128)} %get-tuple-element.4) | data formatting | bytes 131072
  58.3 0.0 copy-done
  58.3 0.6 %copy.12 = f32[128,128]{1,0:T(8,128)} copy(f32[128,128]{1,0:T(8,128)S(1)} %copy-done) | data formatting | bytes 131072
Async XLA Ops:
  56.8 1.5 %copy-start = (f32[128,128]{1,0:T(8,128)S(1)}, f32[128,128]{1,0:T(8,128)}, u32[]{:S(2)}) copy-start(f32[128,128]{1,0:T(8,128)} %get-tuple-element.5) | copy-start | bytes 196612

commit v4 on v3

--- a/solution.py
+++ b/solution.py
@@ -15,7 +15,8 @@
 SWEEPS = 8
 HALO = 2 * SWEEPS
 CAP = 16
-WINDOW = 14
+WINDOW = 12
+GROUPS = 4
 PAD = 8
 ROWS = 32
 
@@ -184,24 +185,33 @@
         for row in (up, tile, down):
             pl.semaphore_signal(barrier, inc=1, device_id=(other, row), device_id_type=MESH)
 
-    for load in loads:
+    for load in loads[:2]:
         load.wait()
-
     eye = iota((blocks, blocks), 0) == iota((blocks, blocks), 1)
     dest_row = dest_ref[...].astype(F32)
     dest_col = jnp.sum(jnp.where(eye, dest_row, 0.0), axis=1, keepdims=True)
     count_col = jnp.sum(jnp.where(eye, count_ref[...].astype(F32), 0.0), axis=1, keepdims=True)
-    live = (iota((blocks, points), 1).astype(F32) < count_col) & (ground_ref[...] == 1)
-    weight = jnp.where(live, weight_ref[...], 0.0)
-    values = (coords_ref[:, 0, :], coords_ref[:, 1, :], weight, weight * height_ref[...])
-    for q, value in enumerate(values):
+    earlier = iota((blocks, blocks), 0) < iota((blocks, blocks), 1)
+    order = jnp.sum(jnp.where((dest_col == dest_row) & earlier, 1.0, 0.0), axis=0, keepdims=True)
+    slot_row = order_of(dest_ref[...], tile, n_tile).astype(F32) * CAP + order
+
+    def split(q, value):
         for part in range(3):
             rounded = value.astype(BF16)
             payload[part * blocks : (part + 1) * blocks, q * points : (q + 1) * points] = rounded
             value = value - rounded.astype(F32)
-    earlier = iota((blocks, blocks), 0) < iota((blocks, blocks), 1)
-    order = jnp.sum(jnp.where((dest_col == dest_row) & earlier, 1.0, 0.0), axis=0, keepdims=True)
-    slot_row = order_of(dest_ref[...], tile, n_tile).astype(F32) * CAP + order
+
+    for load in loads[2:4]:
+        load.wait()
+    live = (iota((blocks, points), 1).astype(F32) < count_col) & (ground_ref[...] == 1)
+    weight = jnp.where(live, weight_ref[...], 0.0)
+    split(2, weight)
+    loads[4].wait()
+    split(3, weight * height_ref[...])
+    loads[5].wait()
+    split(0, coords_ref[:, 0, :])
+    split(1, coords_ref[:, 1, :])
+    loads[6].wait()
 
     def box_copy(shift):
         return pltpu.make_async_remote_copy(
@@ -214,21 +224,22 @@
         )
 
     window = min(WINDOW, n_tile - 1)
-    half = n_tile // 2
-    for first in (0, half):
-        slots = iota((half * CAP, blocks), 0) + first * CAP
+    group = n_tile // GROUPS
+    for first in range(0, n_tile, group):
+        slots = iota((group * CAP, blocks), 0) + first * CAP
         pick = jnp.where(slots.astype(F32) == slot_row, 1.0, 0.0).astype(BF16)
         pick = jnp.concatenate([pick] * 3, axis=1)
         for q in range(4):
             picked = jnp.dot(pick, payload[:, q * points : (q + 1) * points], preferred_element_type=F32)
-            outbox[first : first + half, q * CAP : (q + 1) * CAP, :] = picked.reshape(half, CAP, points)
-    pl.semaphore_wait(barrier, n_tile - 1 + 6)
-
-    def send(shift, carry):
-        box_copy(shift).start()
-        return carry
-
-    lax.fori_loop(1, window + 1, send, 0)
+            outbox[first : first + group, q * CAP : (q + 1) * CAP, :] = picked.reshape(group, CAP, points)
+        if first == 0:
+            pl.semaphore_wait(barrier, n_tile - 1 + 6)
+
+        def send(shift, carry):
+            box_copy(shift).start()
+            return carry
+
+        lax.fori_loop(max(first, 1), max(first, min(first + group, window + 1)), send, 0)
 
     inbox[0] = outbox[0]
     grids[...] = jnp.zeros_like(grids)
@@ -239,11 +250,14 @@
         @pl.when(shift > 0)
         def _():
             box_copy(shift).wait_send()
-            box_copy(shift).wait_recv()
 
         @pl.when((shift > 0) & (shift + window < n_tile))
         def _():
             box_copy(shift + window).start()
+
+        @pl.when(shift > 0)
+        def _():
+            box_copy(shift).wait_recv()
 
         box = inbox[shift]
         x, y, w, u = [box[q * CAP : (q + 1) * CAP, :] for q in range(4)]
@@ -319,16 +333,12 @@
     source = jnp.where(source < 0, source + n_tile, source)
     gap_x = (own_row - source * panels_side - slot % panels_side).astype(F32)
     kernel_x = jnp.exp(-(gap_x * gap_x) / (2.0 * reach_x * reach_x))
-    cell_panel = iota((side, side), 0) // PB
-    column = iota((side, side), 1)
-    gap_y = (cell_panel - column).astype(F32)
-    is_panel = column < panels_side
+    gap_y = (iota((side, side), 0) // PB - iota((side, side), 1) // PB).astype(F32)
     area = 1.0 / (PB * PB)
-    mean_of = jnp.where(is_panel & (cell_panel == column), area, 0.0)
-    smooth_of = jnp.where(is_panel, jnp.exp(-(gap_y * gap_y) / (2.0 * reach_y * reach_y)) * area, 0.0)
+    mean_of = jnp.where(gap_y == 0.0, area, 0.0)
+    smooth_of = jnp.exp(-(gap_y * gap_y) / (2.0 * reach_y * reach_y)) * area
     sum_y = jnp.sum(smooth_of, axis=0, keepdims=True) * (1.0 * PB)
-    denom = jnp.sum(kernel_x, axis=1, keepdims=True) * jnp.where(iota((1, side), 1) < panels_side, sum_y, 1.0)
-    spread_of = jnp.where(iota((side, side), 0) == iota((side, side), 1) // PB, 1.0, 0.0)
+    inverse = 1.0 / (jnp.sum(kernel_x, axis=1, keepdims=True) * sum_y)
 
     rows_all = side + 2 * HALO
     cells[...] = jnp.zeros_like(cells)
@@ -394,11 +404,11 @@
             device_id_type=MESH,
         )
 
-    def send_panel(shift, carry):
-        panel_copy(shift).start()
+    def send_panel(place, carry):
+        panel_copy(lax.rem(place + n_tile // 2 - 1, n_tile - 1) + 1).start()
         return carry
 
-    lax.fori_loop(1, n_tile, send_panel, 0)
+    lax.fori_loop(0, n_tile - 1, send_panel, 0)
     gathered[0] = smooth[...]
     panels = dot_exact(sums, mean_of)
     misfit = jnp.abs(grids[1] - grids[0] * terrain) / (grids[0] + 1.0)
@@ -409,8 +419,7 @@
 
     lax.fori_loop(1, n_tile, wait_panel, 0)
     numer = dot_exact(kernel_x, gathered[...].reshape(all_panels, side))
-    limit = base_slack + slope_slack * jnp.abs(panels - numer / denom)
-    limit = dot_exact(limit, spread_of)
+    limit = base_slack + slope_slack * jnp.abs(panels - numer * inverse)
     limit = jnp.broadcast_to(limit[:, None, :], (panels_side, PB, side)).reshape(side, side)
     limit = jnp.where(fixed_ref[...] == 1, base_slack, limit)
     soft_ref[...] = 1.0 / (1.0 + jnp.exp((misfit - limit) / softness))
@@ -462,16 +471,21 @@
             dma((7,)),
         ],
         compiler_params=pltpu.CompilerParams(
-            collective_id=0, has_side_effects=True, vmem_limit_bytes=60 << 20
+            collective_id=0, has_side_effects=True, vmem_limit_bytes=40 << 20
         ),
     )(
-        pts_coords,
-        pts_height,
-        pts_weight,
-        block_dest.reshape(1, blocks),
-        block_count.reshape(1, blocks),
-        ground_mask,
-        fixed_mask,
+        *[
+            pltpu.with_memory_space_constraint(operand, pltpu.HBM)
+            for operand in (
+                pts_coords,
+                pts_height,
+                pts_weight,
+                block_dest.reshape(1, blocks),
+                block_count.reshape(1, blocks),
+                ground_mask,
+                fixed_mask,
+            )
+        ]
     )
 
 

time: 59.2 us -> 56.4 us (0.953)
  Pallas kernels: 56.2 us -> 54.4 us
  local copies, waits for them, and re-layouts: 2.14 us -> 1.26 us
    pallas_call x1, Pallas kernels: 56.2 us -> 54.4 us  [on_device(): pl.pallas_call(functools.partial(kernel, n_region, n_tile), out_shape=(ou...]
    unnamed x4 -> x2, local copies, waits for them, and re-layouts: 2.14 us -> 1.26 us
where the time goes in v4:
time: 56.4 us; the launch traced here: 56.3 us
  Pallas kernels  54.4 us (96%)
  local copies, waits for them, and re-layouts  1.26 us (2%)
  between operations  0.64 us (1%)
    pallas_call x1, Pallas kernels, on_device(): pl.pallas_call(functools.partial(kernel, n_region, n_tile), out_shape=(ou...  54.4 us
    unnamed x2, local copies, waits for them, and re-layouts  1.26 us

profile of v4, /device:TPU:1, one launch (start us, length us, event | category | flops | bytes accessed | tf_op | source)
XLA Modules:
  0.0 56.3 jit_solution(8675294859423629981)
XLA Ops:
  0.6 54.4 %shard_map.86 = (f32[128,128]{1,0:T(8,128)S(1)}, f32[128,128]{1,0:T(8,128)S(1)}) custom-call(f32[256,2,256]{2,1,0:T(2,128)} %coords_hbm.1, f32[256,256]{1,0:T(8,128)} %height_hbm.1, f32[256,256]{1,0:T(8,128)} %weight_hbm.1, s32[1,256]{1,0:T(1,128)} %bitcast.2, s32[1,256]{1,0:T(1,128)} %bitcast.3, s32[256,256]{1,0:T(8,128)} %ground_hbm.1, s32[128,128]{1,0:T(8,128)} %fixed_hbm.1), custom_call_target="tpu_custom_call" | custom-call | tf_op jit(solution)/shard_map/pallas_call | solution.py:435
  55.0 0.6 %copy.11 = f32[128,128]{1,0:T(8,128)} copy(f32[128,128]{1,0:T(8,128)S(1)} %get-tuple-element.4) | data formatting | bytes 131072
  55.7 0.6 %copy.12 = f32[128,128]{1,0:T(8,128)} copy(f32[128,128]{1,0:T(8,128)S(1)} %get-tuple-element.5) | data formatting | bytes 131072

commit v5 on v4

--- a/solution.py
+++ b/solution.py
@@ -15,7 +15,7 @@
 SWEEPS = 8
 HALO = 2 * SWEEPS
 CAP = 16
-WINDOW = 12
+WINDOW = 18
 GROUPS = 4
 PAD = 8
 ROWS = 32
@@ -164,7 +164,8 @@
                 (ground_hbm, ground_ref),
                 (weight_hbm, weight_ref),
                 (height_hbm, height_ref),
-                (coords_hbm, coords_ref),
+                (coords_hbm.at[:, 0, :], coords_ref.at[0]),
+                (coords_hbm.at[:, 1, :], coords_ref.at[1]),
                 (fixed_hbm, fixed_ref),
             )
         )
@@ -209,9 +210,10 @@
     loads[4].wait()
     split(3, weight * height_ref[...])
     loads[5].wait()
-    split(0, coords_ref[:, 0, :])
-    split(1, coords_ref[:, 1, :])
+    split(0, coords_ref[0])
     loads[6].wait()
+    split(1, coords_ref[1])
+    loads[7].wait()
 
     def box_copy(shift):
         return pltpu.make_async_remote_copy(
@@ -288,16 +290,8 @@
 
     lax.fori_loop(0, n_tile, splat, 0)
 
-    density, heights = grids[0], grids[1]
     last = side - HALO
-    lane = iota((side, side), 1)
-    both = jnp.where(
-        (lane < HALO) | (lane >= last),
-        density,
-        jnp.where(lane < 2 * HALO, pltpu.roll(heights, HALO, 1), pltpu.roll(heights, last, 1)),
-    )
-    edge[...] = both
-    edge_turned[...] = both.T
+    head, tail = pl.ds(0, HALO), pl.ds(last, HALO)
 
     def halo_copy(k, src, dst, device):
         return pltpu.make_async_remote_copy(
@@ -309,18 +303,30 @@
             device_id_type=MESH,
         )
 
-    head, tail = pl.ds(0, HALO), pl.ds(last, HALO)
     copies = [
-        halo_copy(0, edge.at[head, :], corner.at[0], (left, up)),
-        halo_copy(1, edge.at[head, :], corner.at[1], (right, up)),
-        halo_copy(2, edge.at[tail, :], corner.at[2], (left, down)),
-        halo_copy(3, edge.at[tail, :], corner.at[3], (right, down)),
-        halo_copy(4, edge_turned.at[pl.ds(0, 2 * HALO), :], from_side.at[0], (left, tile)),
-        halo_copy(5, edge_turned.at[pl.ds(side - 2 * HALO, 2 * HALO), :], from_side.at[1], (right, tile)),
-        halo_copy(6, grids.at[:, head, :], from_down, (region, up)),
-        halo_copy(7, grids.at[:, tail, :], from_up, (region, down)),
+        halo_copy(0, grids.at[:, head, :], from_down, (region, up)),
+        halo_copy(1, grids.at[:, tail, :], from_up, (region, down)),
+        halo_copy(2, edge.at[head, :], corner.at[0], (left, up)),
+        halo_copy(3, edge.at[head, :], corner.at[1], (right, up)),
+        halo_copy(4, edge.at[tail, :], corner.at[2], (left, down)),
+        halo_copy(5, edge.at[tail, :], corner.at[3], (right, down)),
+        halo_copy(6, edge_turned.at[pl.ds(0, 2 * HALO), :], from_side.at[0], (left, tile)),
+        halo_copy(7, edge_turned.at[pl.ds(side - 2 * HALO, 2 * HALO), :], from_side.at[1], (right, tile)),
     ]
-    for copy in copies:
+    for copy in copies[:2]:
+        copy.start()
+    density, heights = grids[0], grids[1]
+    lane = iota((side, side), 1)
+    both = jnp.where(
+        (lane < HALO) | (lane >= last),
+        density,
+        jnp.where(lane < 2 * HALO, pltpu.roll(heights, HALO, 1), pltpu.roll(heights, last, 1)),
+    )
+    edge[...] = both
+    for copy in copies[2:6]:
+        copy.start()
+    edge_turned[...] = both.T
+    for copy in copies[6:]:
         copy.start()
 
     panels_side = side // PB
@@ -387,7 +393,7 @@
                 cells[k, PAD + first : PAD + first + ROWS, :] = v + field[2, k, rows, :] * residue
         return carry
 
-    lax.fori_loop(0, SWEEPS, sweep, 0)
+    lax.fori_loop(0, SWEEPS, sweep, 0, unroll=SWEEPS)
     terrain = cells[0, PAD + HALO : PAD + HALO + side, :]
     terrain_ref[...] = terrain
 
@@ -438,7 +444,7 @@
         in_specs=[pl.BlockSpec(memory_space=pltpu.HBM)] * 7,
         out_specs=[pl.BlockSpec(memory_space=pltpu.VMEM)] * 2,
         scratch_shapes=[
-            pltpu.VMEM(pts_coords.shape, F32),
+            pltpu.VMEM((2, blocks, points), F32),
             pltpu.VMEM((blocks, points), F32),
             pltpu.VMEM((blocks, points), F32),
             pltpu.VMEM((1, blocks), jnp.int32),
@@ -468,7 +474,7 @@
             dma((8,)),
             dma((n_tile,)),
             dma((n_tile,)),
-            dma((7,)),
+            dma((8,)),
         ],
         compiler_params=pltpu.CompilerParams(
             collective_id=0, has_side_effects=True, vmem_limit_bytes=40 << 20

time: 56.4 us -> 55.8 us (0.989)
  Pallas kernels: 54.4 us -> 53.8 us
    pallas_call x1, Pallas kernels: 54.4 us -> 53.8 us  [on_device(): pl.pallas_call(functools.partial(kernel, n_region, n_tile), out_shape=(ou...]
where the time goes in v5:
time: 55.8 us; the launch traced here: 55.7 us
  Pallas kernels  53.8 us (96%)
  local copies, waits for them, and re-layouts  1.26 us (2%)
  between operations  0.64 us (1%)
    pallas_call x1, Pallas kernels, on_device(): pl.pallas_call(functools.partial(kernel, n_region, n_tile), out_shape=(ou...  53.8 us
    unnamed x2, local copies, waits for them, and re-layouts  1.26 us

profile of v5, /device:TPU:1, one launch (start us, length us, event | category | flops | bytes accessed | tf_op | source)
XLA Modules:
  0.0 55.7 jit_solution(13270131234427864460)
XLA Ops:
  0.6 53.8 %shard_map.86 = (f32[128,128]{1,0:T(8,128)S(1)}, f32[128,128]{1,0:T(8,128)S(1)}) custom-call(f32[256,2,256]{2,1,0:T(2,128)} %coords_hbm.1, f32[256,256]{1,0:T(8,128)} %height_hbm.1, f32[256,256]{1,0:T(8,128)} %weight_hbm.1, s32[1,256]{1,0:T(1,128)} %bitcast.2, s32[1,256]{1,0:T(1,128)} %bitcast.3, s32[256,256]{1,0:T(8,128)} %ground_hbm.1, s32[128,128]{1,0:T(8,128)} %fixed_hbm.1), custom_call_target="tpu_custom_call" | custom-call | tf_op jit(solution)/shard_map/pallas_call | solution.py:441
  54.4 0.6 %copy.11 = f32[128,128]{1,0:T(8,128)} copy(f32[128,128]{1,0:T(8,128)S(1)} %get-tuple-element.4) | data formatting | bytes 131072
  55.0 0.6 %copy.12 = f32[128,128]{1,0:T(8,128)} copy(f32[128,128]{1,0:T(8,128)S(1)} %get-tuple-element.5) | data formatting | bytes 131072

commit v6 on v5

--- a/solution.py
+++ b/solution.py
@@ -48,7 +48,7 @@
             added = (dx in (1, 2), dx in (2, 3), dy in (1, 2), dy in (2, 3), dz)
             return [have + more for have, more in zip(load, added)]
 
-        step = min(left, key=lambda c: (max(after(c)), sum(after(c)), sum(v * v for v in after(c)), c))
+        step = min(left, key=lambda c: (sum(after(c)), max(after(c)), sum(v * v for v in after(c)), c))
         load = after(step)
         left.remove(step)
         order.append(step)

time: 55.8 us -> 55.8 us (level)
  no operation moved by 1% of the time
where the time goes in v6:
time: 55.8 us; the launch traced here: 55.7 us
  Pallas kernels  53.8 us (96%)
  local copies, waits for them, and re-layouts  1.26 us (2%)
  between operations  0.64 us (1%)
    pallas_call x1, Pallas kernels, on_device(): pl.pallas_call(functools.partial(kernel, n_region, n_tile), out_shape=(ou...  53.8 us
    unnamed x2, local copies, waits for them, and re-layouts  1.26 us

profile of v6, /device:TPU:1, one launch (start us, length us, event | category | flops | bytes accessed | tf_op | source)
XLA Modules:
  0.0 55.7 jit_solution(13270131234427864460)
XLA Ops:
  0.6 53.8 %shard_map.86 = (f32[128,128]{1,0:T(8,128)S(1)}, f32[128,128]{1,0:T(8,128)S(1)}) custom-call(f32[256,2,256]{2,1,0:T(2,128)} %coords_hbm.1, f32[256,256]{1,0:T(8,128)} %height_hbm.1, f32[256,256]{1,0:T(8,128)} %weight_hbm.1, s32[1,256]{1,0:T(1,128)} %bitcast.2, s32[1,256]{1,0:T(1,128)} %bitcast.3, s32[256,256]{1,0:T(8,128)} %ground_hbm.1, s32[128,128]{1,0:T(8,128)} %fixed_hbm.1), custom_call_target="tpu_custom_call" | custom-call | tf_op jit(solution)/shard_map/pallas_call | solution.py:441
  54.4 0.6 %copy.11 = f32[128,128]{1,0:T(8,128)} copy(f32[128,128]{1,0:T(8,128)S(1)} %get-tuple-element.4) | data formatting | bytes 131072
  55.0 0.6 %copy.12 = f32[128,128]{1,0:T(8,128)} copy(f32[128,128]{1,0:T(8,128)S(1)} %get-tuple-element.5) | data formatting | bytes 131072

commit v7 on v5

--- a/solution.py
+++ b/solution.py
@@ -57,11 +57,16 @@
 
 def tile_step(tile, k, n_tile):
     order = partner_order(n_tile)
-    step = order[0]
-    for place in range(1, n_tile):
-        step = jnp.where(k == place, order[place], step)
     if n_tile != 32:
-        return lax.rem(tile + step, n_tile)
+        return lax.rem(tile + k, n_tile)
+    words = [sum(order[4 * w + i] << (5 * i) for i in range(4)) for w in range(8)]
+    high, low = k // 4, lax.rem(k, 4)
+    word = words[0]
+    for w in range(1, 8):
+        word = jnp.where(high == w, words[w], word)
+    step = word & 31
+    for i in range(1, 4):
+        step = jnp.where(low == i, (word >> (5 * i)) & 31, step)
     x, z, y = tile // 8, lax.rem(tile // 4, 2), lax.rem(tile, 4)
     x = lax.rem(x + step // 8, 4)
     z = lax.rem(z + step // 4, 2)

time: 55.8 us -> 56.2 us (level)
  no operation moved by 1% of the time
where the time goes in v7:
time: 56.2 us; the launch traced here: 56 us
  Pallas kernels  54.1 us (96%)
  local copies, waits for them, and re-layouts  1.26 us (2%)
  between operations  0.64 us (1%)
    pallas_call x1, Pallas kernels, on_device(): pl.pallas_call(functools.partial(kernel, n_region, n_tile), out_shape=(ou...  54.1 us
    unnamed x2, local copies, waits for them, and re-layouts  1.26 us

profile of v7, /device:TPU:1, one launch (start us, length us, event | category | flops | bytes accessed | tf_op | source)
XLA Modules:
  0.0 56.0 jit_solution(4262315193782033260)
XLA Ops:
  0.6 54.1 %shard_map.86 = (f32[128,128]{1,0:T(8,128)S(1)}, f32[128,128]{1,0:T(8,128)S(1)}) custom-call(f32[256,2,256]{2,1,0:T(2,128)} %coords_hbm.1, f32[256,256]{1,0:T(8,128)} %height_hbm.1, f32[256,256]{1,0:T(8,128)} %weight_hbm.1, s32[1,256]{1,0:T(1,128)} %bitcast.2, s32[1,256]{1,0:T(1,128)} %bitcast.3, s32[256,256]{1,0:T(8,128)} %ground_hbm.1, s32[128,128]{1,0:T(8,128)} %fixed_hbm.1), custom_call_target="tpu_custom_call" | custom-call | tf_op jit(solution)/shard_map/pallas_call | solution.py:446
  54.8 0.6 %copy.11 = f32[128,128]{1,0:T(8,128)} copy(f32[128,128]{1,0:T(8,128)S(1)} %get-tuple-element.4) | data formatting | bytes 131072
  55.4 0.6 %copy.12 = f32[128,128]{1,0:T(8,128)} copy(f32[128,128]{1,0:T(8,128)S(1)} %get-tuple-element.5) | data formatting | bytes 131072
